TPU v7x, 128 devices: a whole 4x4x4 slice. The times are simulated.
128 devices in a mesh: bundle: 64 (over x, y, z), elem: 2 (over core).
Axes of the slice: x: 4, y: 4, z: 4, core: 2. Of those that a mesh axis runs over, the one named last changes fastest.
Arguments:
- volt_start: float32 [16384, 2048], P(('bundle', 'elem')), may hold values from -6 to 6
- seg_ids: int32 [16384, 2048], P(('bundle', 'elem')), may hold values from 0 to 7, never falling along the last dimension, each value on 1 to 512 neighbouring positions
- cond_table: float32 [8], replicated, may hold values from 0.05 to 0.45
- tile_owner: int32 [262144, 1], P(('bundle', 'elem')), may hold values from 0 to 127; in each aligned block of 2048 rows (0 to 2047, 2048 to 4095, ...) at most 32 rows name the same one
- tile_elem: int32 [262144], P(('bundle', 'elem')), may hold values from 0 to 511
- material: bfloat16 [128, 128], replicated, may hold values from -0.1875 to 0.1875
- stress_cot: float32 [65536, 128], P(('bundle', 'elem')), may hold values from -6 to 6
Outputs:
- volt_grad: float32 [16384, 2048], P(('bundle', 'elem'))
- stress: float32 [65536, 128], P(('bundle', 'elem'))
- material_grad: float32 [128, 128], replicated
- cond_grad: float32 [8], replicated
Inputs may be any that keep to these rules, and one draw needn't show every extreme that they name: `tile_owner`: in the rows of one device (aligned blocks of 2048 rows) no owner is named more than 32 times, a bound that some block reaches. `seg_ids`: never falls along a fiber; a segment spans at most 512 nodes.
All inputs are finite; a program needn't handle non-finite values.
Results may differ from a plain program's by a relative error of at most 0.0048.
Values may be sent and summed in bfloat16 or wider, within the bound.
No kernel may reach another device: no remote copies, remote signals or barrier semaphores. Data moves between devices by JAX's collectives and lax.ppermute only.
A program may use at most 64 MiB of HBM per device.

v0:
```python
import jax
import jax.numpy as jnp
from jax import lax
from jax.sharding import PartitionSpec as P

SEGS = 8
STEPS = 4


time_step = 0.5
react_gain = 1.5


def fiber_step(volts, condn):
    left = jnp.concatenate([volts[:, :1], volts[:, :-1]], axis=1)
    right = jnp.concatenate([volts[:, 1:], volts[:, -1:]], axis=1)
    return volts + time_step * (
        condn * (left - 2.0 * volts + right) + jnp.tanh(react_gain * volts) - volts
    )


def send_tiles(send_buf, send_ids, n_bundle, n_elem, capacity):
    width = send_buf.shape[-1]
    got_buf, got_ids = (
        lax.all_to_all(
            send_buf.reshape(n_bundle * n_elem, capacity, width),
            ("bundle", "elem"),
            split_axis=0,
            concat_axis=0,
            tiled=True,
        ),
        lax.all_to_all(
            send_ids.reshape(n_bundle * n_elem, capacity),
            ("bundle", "elem"),
            split_axis=0,
            concat_axis=0,
            tiled=True,
        ),
    )
    return (got_buf.reshape(-1, width), got_ids.reshape(-1))


def return_grads(back_buf, n_bundle, n_elem, capacity):
    width = back_buf.shape[-1]
    got_back = lax.all_to_all(
        back_buf.reshape(n_bundle * n_elem, capacity, width),
        ("bundle", "elem"),
        split_axis=0,
        concat_axis=0,
        tiled=True,
    )
    return got_back.reshape(-1, width)


def per_device(volt_start, seg_ids, cond_table, tile_owner, tile_elem, material, stress_cot):
    fibers_here, nodes_count = volt_start.shape
    width = material.shape[0]
    tiles_per = nodes_count // width
    n_bundle = lax.axis_size("bundle")
    n_elem = lax.axis_size("elem")
    owners_count = n_bundle * n_elem
    tiles_here = fibers_here * tiles_per
    capacity = max(2, 2 * tiles_here // owners_count)
    elems_here = stress_cot.shape[0]
    condn = jnp.zeros(volt_start.shape, jnp.float32)
    for segment in range(SEGS):
        condn = jnp.where(seg_ids == segment, cond_table[segment], condn)
    states = [volt_start]
    volts = volt_start
    for index in range(STEPS):
        volts = fiber_step(volts, condn)
        states.append(volts)
    tanh_end = jnp.tanh(volts)
    act_tiles = tanh_end.astype(jnp.bfloat16).reshape(tiles_here, width)
    owner_col = tile_owner[:, 0]
    onehot = (owner_col[:, None] == jnp.arange(owners_count, dtype=jnp.int32)[None, :]).astype(
        jnp.int32
    )
    placed = jnp.sum(jnp.cumsum(onehot, axis=0) * onehot, axis=1) - 1
    slot_index = owner_col * capacity + placed
    send_buf = (
        jnp.zeros((owners_count * capacity, width), jnp.bfloat16).at[slot_index].set(act_tiles)
    )
    send_ids = (
        jnp.full((owners_count * capacity,), elems_here, jnp.int32).at[slot_index].set(tile_elem)
    )
    got_buf, got_ids = send_tiles(send_buf, send_ids, n_bundle, n_elem, capacity)
    summed = jax.ops.segment_sum(got_buf.astype(jnp.float32), got_ids, num_segments=elems_here + 1)[
        :elems_here
    ]
    summed_b = summed.astype(jnp.bfloat16)
    stress = jnp.tanh(jnp.dot(summed_b, material, preferred_element_type=jnp.float32))
    gpre = stress_cot * (1.0 - stress * stress)
    gsum = jnp.dot(gpre, material.astype(jnp.float32).T, precision=lax.Precision.HIGHEST)
    local_mat = jnp.dot(summed_b.astype(jnp.float32).T, gpre, precision=lax.Precision.HIGHEST)
    gsum_ext = jnp.concatenate([gsum, jnp.zeros((1, width), jnp.float32)], axis=0)
    back_buf = gsum_ext[got_ids]
    got_back = return_grads(back_buf, n_bundle, n_elem, capacity)
    tile_grad = got_back[slot_index]
    grad_now = tile_grad.reshape(fibers_here, nodes_count) * (1.0 - tanh_end * tanh_end)
    condn_grad = jnp.zeros(volt_start.shape, jnp.float32)
    for index in reversed(range(STEPS)):
        before = states[index]
        unused, puller = jax.vjp(fiber_step, before, condn)
        grad_now, cond_part = puller(grad_now)
        condn_grad = condn_grad + cond_part
    local_cond = jnp.stack(
        [jnp.sum(jnp.where(seg_ids == segment, condn_grad, 0.0)) for segment in range(SEGS)]
    )
    material_grad, cond_grad = lax.psum((local_mat, local_cond), ("bundle", "elem"))
    return (grad_now, stress, material_grad, cond_grad)


def solution(mesh):
    return jax.shard_map(
        per_device,
        mesh=mesh,
        in_specs=(
            P(("bundle", "elem"), None),
            P(("bundle", "elem"), None),
            P(),
            P(("bundle", "elem"), None),
            P(("bundle", "elem")),
            P(),
            P(("bundle", "elem"), None),
        ),
        out_specs=(P(("bundle", "elem"), None), P(("bundle", "elem"), None), P(), P()),
        check_vma=False,
    )
```

profile of v0, /device:TPU:1, one launch (start us, length us, event | category | flops | bytes accessed | tf_op | source)
XLA Modules:
  0.0 286.3 jit_solution(9305132579134023986)
XLA Ops:
  7.2 0.8 copy.14
  8.0 0.3 fusion.7
  8.5 0.3 copy.15
  9.1 0.6 fusion.6
  9.7 8.2 %scatter_custom_fusion = s32[4096]{0:T(1024)S(1)} fusion(s32[2048]{0:T(1024)S(1)} %bitcast.47, s32[2048]{0:T(1024)} %param.11, s32[]{:T(128)} %constant.22.clone.1), kind=kCustom, calls=%fused_computation.70 | custom fusion | bytes 16896 | tf_op jit(solution)/shard_map/scatter | solution.py:85
  18.0 0.7 all_to_all.12
  18.7 11.5 %all-to-all-start = ((s32[128,1,32]{2,1,0:T(1,128)}), s32[128,1,32]{2,1,0:T(1,128)S(1)}, u32[]{:S(2)}, u32[]{:S(2)}) async-start(s32[128,1,32]{2,1,0:T(1,128)} %bitcast.7), calls=%async_computation | async-start | bytes 131072 | tf_op jit(solution)/shard_map/all_to_all | solution.py:32
  30.3 0.4 fusion.31
  31.0 0.8 fusion.32
  31.7 8.0 %multiply_add_fusion.3 = (f32[128,2048]{1,0:T(8,128)S(1)}, f32[128,2048]{1,0:T(8,128)S(1)}, pred[128,2048]{1,0:T(8,128)(4,1)}, pred[128,2048]{1,0:T(8,128)(4,1)}...) fusion(f32[128,2048]{1,0:T(8,128)S(1)} %copy-done.5, ...), kind=kLoop, calls=%fused_computation.42 | loop fusion | flops 7077888 | bytes 8388640 | tf_op jit(solution)/shard_map/add | solution.py:17
  39.9 0.4 fusion.29
  40.3 0.5 copy-done.7
  40.8 0.6 multiply_add_fusion.2
  41.7 0.4 fusion.27
  42.0 0.5 copy-done.3
  42.6 0.5 multiply_add_fusion.1
  43.5 0.4 fusion.25
  43.9 0.5 copy-done.1
  44.5 1.6 fusion.19
  46.3 6.8 %scatter_custom_fusion.1 = bf16[4096,128]{1,0:T(8,128)(2,1)} fusion(s32[2048]{0:T(1024)S(1)} %bitcast.48, bf16[2048,128]{1,0:T(8,128)(2,1)S(1)} %reshape.121, bf16[]{:T(256)} %constant.8.clone.1), kind=kCustom, calls=%fused_computation.57 | custom fusion | bytes 1048578 | tf_op jit(solution)/shard_map/scatter | solution.py:82
  53.1 9.8 %all-to-all-start.1 = ((bf16[128,32,128]{2,1,0:T(8,128)(2,1)}), bf16[128,32,128]{2,1,0:T(8,128)(2,1)S(1)}, u32[]{:S(2)}, u32[]{:S(2)}) async-start(bf16[128,32,128]{2,1,0:T(8,128)(2,1)} %bitcast.16), calls=%async_computation.1 | async-start | bytes 2097152 | tf_op jit(solution)/shard_map/all_to_all | solution.py:25
  63.0 0.5 broadcast.241
  63.5 0.8 reduce.5
  64.4 17.7 %all-to-all-done.1 = bf16[128,32,128]{2,1,0:T(8,128)(2,1)S(1)} async-done(((bf16[128,32,128]{2,1,0:T(8,128)(2,1)}), bf16[128,32,128]{2,1,0:T(8,128)(2,1)S(1)}, u32[]{:S(2)}, u32[]{:S(2)}) %all-to-all-start.1) | async-done | bytes 1048608 | tf_op jit(solution)/shard_map/all_to_all | solution.py:25
  82.2 22.6 %scatter_custom_fusion.2 = f32[513,128]{1,0:T(8,128)S(1)} fusion(s32[4096]{0:T(1024)S(1)} %reshape.127, bf16[4096,128]{1,0:T(8,128)(2,1)S(1)} %bitcast.42, f32[]{:T(128)} %constant.21.clone.1), kind=kCustom, calls=%fused_computation.5 | custom fusion | flops 1048576 | bytes 1311236 | tf_op jit(solution)/shard_map/scatter-add | solution.py:88
  105.3 14.1 %gather_fusion = f32[4096,128]{1,0:T(8,128)} fusion(f32[513,128]{1,0:T(8,128)S(1)} %concatenate.43, s32[4096]{0:T(1024)S(1)} %broadcast_clamp_fusion), kind=kCustom, calls=%fused_computation | custom fusion | bytes 4210688 | tf_op jit(solution)/shard_map/gather | solution.py:97
  119.4 5.8 %all-to-all-start.2 = ((f32[128,32,128]{2,1,0:T(8,128)}), f32[128,32,128]{2,1,0:T(8,128)S(1)}, u32[]{:S(2)}, u32[]{:S(2)}) async-start(f32[128,32,128]{2,1,0:T(8,128)} %bitcast.41), calls=%async_computation.2 | async-start | bytes 4194304 | tf_op jit(solution)/shard_map/all_to_all | solution.py:45
  125.3 2.0 fusion.13
  127.3 28.5 %all-to-all-done.2 = f32[128,32,128]{2,1,0:T(8,128)S(1)} async-done(((f32[128,32,128]{2,1,0:T(8,128)}), f32[128,32,128]{2,1,0:T(8,128)S(1)}, u32[]{:S(2)}, u32[]{:S(2)}) %all-to-all-start.2) | async-done | bytes 2097184 | tf_op jit(solution)/shard_map/all_to_all | solution.py:45
  155.8 7.5 %gather_fusion.1 = f32[2048,128]{1,0:T(8,128)} fusion(f32[4096,128]{1,0:T(8,128)S(1)} %bitcast.40, s32[2048]{0:T(1024)S(1)} %broadcast_clamp_fusion.1), kind=kCustom, calls=%fused_computation.1 | custom fusion | bytes 2105344 | tf_op jit(solution)/shard_map/gather | solution.py:99
  163.3 1.5 reshape.91
  165.2 0.4 fusion.23
  165.5 0.9 copy-done.2
  166.4 0.9 multiply_multiply_fusion.2
  167.4 0.4 fusion.22
  167.7 0.8 copy-done.4
  168.6 0.8 multiply_multiply_fusion.1
  169.6 0.4 fusion.21
  170.7 0.3 copy-done.22
  171.7 0.6 copy-done.6
  173.2 3.2 %multiply_add_fusion = (f32[128,2048]{1,0:T(8,128)S(1)}, f32[128,2048]{1,0:T(8,128)S(1)}) fusion(f32[128,2048]{1,0:T(8,128)S(1)} %get-tuple-element.15, f32[128,2048]{1,0:T(8,128)S(1)} %get-tuple-element.17, f32[128,1]{1,0:T(8,128)S(1)} %copy-done.54, f32[128,2047]{1,0:T(8,128)S(1)} %copy-done.22, f32[128,2048]{1,0:T(8,128)S(1)} %copy-done.2, ...), kind=kLoop, calls=%fused_computation.26 | loop fusion | flops 13631488 | bytes 22021632 | tf_op jit(solution)/shard_map/add | solution.py:106
  176.5 2.0 select_reduce_fusion
  178.5 1.7 fusion.20
  180.3 5.2 %stack.35 = f32[8]{0:T(128)S(1)} concatenate(f32[1]{0:T(128)} %bitcast.21, f32[1]{0:T(128)} %bitcast.22, f32[1]{0:T(128)} %bitcast.23, f32[1]{0:T(128)} %bitcast.24, f32[1]{0:T(128)} %bitcast.25, f32[1]{0:T(128)} %bitcast.26, f32[1]{0:T(128)} %bitcast.27, f32[1]{0:T(128)} %bitcast.28), dimensions={0} | concatenate | bytes 64 | tf_op jit(solution)/shard_map/stack | solution.py:107
  185.4 3.2 %select_add_fusion = f32[128,2048]{1,0:T(8,128)} fusion(f32[128,2047]{1,0:T(8,128)} %get-tuple-element.31, f32[128,2047]{1,0:T(8,128)} %get-tuple-element.30, f32[128,1]{1,0:T(8,128)S(1)} %split.61, f32[128,2048]{1,0:T(8,128)S(1)} %copy-done.24, f32[128,2048]{1,0:T(8,128)S(1)} %copy-done.6, pred[2048]{0:T(1024)(128)(4,1)S(1)} %copy-done.57, ...), kind=kLoop, calls=%fused_computation.27 | loop fusion | flops 4980736 | bytes 6292992 | tf_op jit(solution)/shard_map/transpose(jvp())/add_any | solution.py:15
  188.7 63.0 %psum.15 = f32[8]{0:T(128)} all-reduce(f32[8]{0:T(128)S(1)} %stack.35), channel_id=1, replica_groups=mesh['bundle'=64,'elem'=2] {'bundle','elem'}, use_global_device_ids=true, to_apply=%region_15.16 | all-reduce | flops 8 | bytes 64 | tf_op jit(solution)/shard_map/psum | solution.py:110
  251.7 26.3 %all-reduce.15.cloned.1.call-done = f32[128,128]{1,0:T(8,128)} async-done(((f32[128,128]{1,0:T(8,128)}), f32[128,128]{1,0:T(8,128)}) %all-reduce.15.cloned.1.call-update) | async-done | bytes 65552 | tf_op jit(solution)/shard_map/psum | solution.py:110
  277.9 1.5 copy.18
  (136 shorter events, 5.6 us)
Async XLA Ops:
  7.2 97.6 %copy-start = (bf16[128,128]{1,0:T(8,128)(2,1)S(1)}, bf16[128,128]{1,0:T(8,128)(2,1)}, u32[]{:S(2)}) copy-start(bf16[128,128]{1,0:T(8,128)(2,1)} %param.12) | copy-start | bytes 98308
  8.5 21.7 %copy-start.5 = (f32[128,2048]{1,0:T(8,128)S(1)}, f32[128,2048]{1,0:T(8,128)}, u32[]{:S(2)}) copy-start(f32[128,2048]{1,0:T(8,128)} %param.7) | copy-start | bytes 3145732
  18.7 34.4 %all-to-all-start = ((s32[128,1,32]{2,1,0:T(1,128)}), s32[128,1,32]{2,1,0:T(1,128)S(1)}, u32[]{:S(2)}, u32[]{:S(2)}) async-start(s32[128,1,32]{2,1,0:T(1,128)} %bitcast.7), calls=%async_computation | async-start | bytes 131072 | tf_op jit(solution)/shard_map/all_to_all | solution.py:32
  30.3 1.4 copy-start.41
  30.3 1.4 copy-start.32
  30.9 8.8 %copy-start.25 = (f32[128,2047]{1,0:T(8,128)}, f32[128,2047]{1,0:T(8,128)S(1)}, u32[]{:S(2)}) copy-start(f32[128,2047]{1,0:T(8,128)S(1)} %get-tuple-element.52) | copy-start | bytes 3144196
  30.9 8.8 %copy-start.27 = (f32[128,2047]{1,0:T(8,128)}, f32[128,2047]{1,0:T(8,128)S(1)}, u32[]{:S(2)}) copy-start(f32[128,2047]{1,0:T(8,128)S(1)} %get-tuple-element.53) | copy-start | bytes 3144196
  40.3 1.3 copy-start.13
  42.0 1.4 copy-start.17
  43.9 2.1 copy-start.19
  43.9 2.1 copy-start.21
  53.1 51.9 %copy-start.31 = (f32[512,128]{1,0:T(8,128)S(1)}, f32[512,128]{1,0:T(8,128)}, u32[]{:S(2)}) copy-start(f32[512,128]{1,0:T(8,128)} %param.13) | copy-start | bytes 786436
  53.1 29.0 %all-to-all-start.1 = ((bf16[128,32,128]{2,1,0:T(8,128)(2,1)}), bf16[128,32,128]{2,1,0:T(8,128)(2,1)S(1)}, u32[]{:S(2)}, u32[]{:S(2)}) async-start(bf16[128,32,128]{2,1,0:T(8,128)(2,1)} %bitcast.16), calls=%async_computation.1 | async-start | bytes 2097152 | tf_op jit(solution)/shard_map/all_to_all | solution.py:25
  104.8 14.6 %copy-start.30 = (f32[513,128]{1,0:T(8,128)}, f32[513,128]{1,0:T(8,128)S(1)}, u32[]{:S(2)}) copy-start(f32[513,128]{1,0:T(8,128)S(1)} %scatter_custom_fusion.2) | copy-start | bytes 787972
  105.0 20.3 %copy-start.29 = (f32[512,128]{1,0:T(8,128)}, f32[512,128]{1,0:T(8,128)S(1)}, u32[]{:S(2)}) copy-start(f32[512,128]{1,0:T(8,128)S(1)} %convolution_tanh_fusion) | copy-start | bytes 786436
  119.4 36.4 %all-to-all-start.2 = ((f32[128,32,128]{2,1,0:T(8,128)}), f32[128,32,128]{2,1,0:T(8,128)S(1)}, u32[]{:S(2)}, u32[]{:S(2)}) async-start(f32[128,32,128]{2,1,0:T(8,128)} %bitcast.41), calls=%async_computation.2 | async-start | bytes 4194304 | tf_op jit(solution)/shard_map/all_to_all | solution.py:45
  125.2 152.7 %all-reduce.15.cloned.1.call-start = ((), (), s32[]{:S(2)}) async-start(), calls=%async_computation.3 | async-start | bytes 131072 | tf_op jit(solution)/shard_map/psum | solution.py:110
  163.3 1.6 copy-start.9
  165.2 1.2 copy-start.2
  167.3 1.2 copy-start.4
  167.3 2.6 copy-start.48
  167.3 2.6 copy-start.50
  167.4 2.6 copy-start.52
  167.4 2.6 copy-start.54
  168.6 1.4 copy-start.14
  168.6 1.5 copy-start.16
  168.6 1.9 copy-start.18
  168.6 2.2 copy-start.20
  168.6 2.5 copy-start.22
  168.6 2.8 copy-start.26
  168.6 3.1 %copy-start.28 = (f32[128,2047]{1,0:T(8,128)S(1)}, f32[128,2047]{1,0:T(8,128)}, u32[]{:S(2)}) copy-start(f32[128,2047]{1,0:T(8,128)} %copy-done.27) | copy-start | bytes 3144196
  168.6 3.1 %copy-start.42 = (f32[128,1]{1,0:T(8,128)S(1)}, f32[128,1]{1,0:T(8,128)}, u32[]{:S(2)}) copy-start(f32[128,1]{1,0:T(8,128)} %copy-done.41) | copy-start | bytes 1540
  168.6 3.1 %copy-start.44 = (f32[128,1]{1,0:T(8,128)S(1)}, f32[128,1]{1,0:T(8,128)}, u32[]{:S(2)}) copy-start(f32[128,1]{1,0:T(8,128)} %copy-done.43) | copy-start | bytes 1540
  168.6 3.1 %copy-start.46 = (f32[128,1]{1,0:T(8,128)S(1)}, f32[128,1]{1,0:T(8,128)}, u32[]{:S(2)}) copy-start(f32[128,1]{1,0:T(8,128)} %copy-done.45) | copy-start | bytes 1540
  169.5 2.7 copy-start.6
  169.5 3.0 %copy-start.8 = (f32[128,2048]{1,0:T(8,128)S(1)}, f32[128,2048]{1,0:T(8,128)}, u32[]{:S(2)}) copy-start(f32[128,2048]{1,0:T(8,128)} %copy-done.7) | copy-start | bytes 3145732
  169.5 3.3 %copy-start.10 = (f32[128,2048]{1,0:T(8,128)S(1)}, f32[128,2048]{1,0:T(8,128)}, u32[]{:S(2)}) copy-start(f32[128,2048]{1,0:T(8,128)} %get-tuple-element.19) | copy-start | bytes 3145732
  169.6 3.6 %copy-start.12 = (f32[128,2047]{1,0:T(8,128)S(1)}, f32[128,2047]{1,0:T(8,128)}, u32[]{:S(2)}) copy-start(f32[128,2047]{1,0:T(8,128)} %copy-done.11) | copy-start | bytes 3144196
  173.2 3.3 %copy-start.33 = (pred[128,2048]{1,0:T(8,128)(4,1)S(1)}, pred[128,2048]{1,0:T(8,128)(4,1)}, u32[]{:S(2)}) copy-start(pred[128,2048]{1,0:T(8,128)(4,1)} %get-tuple-element.22) | copy-start | bytes 786436
  173.2 3.3 %copy-start.34 = (pred[128,2048]{1,0:T(8,128)(4,1)S(1)}, pred[128,2048]{1,0:T(8,128)(4,1)}, u32[]{:S(2)}) copy-start(pred[128,2048]{1,0:T(8,128)(4,1)} %get-tuple-element.23) | copy-start | bytes 786436
  173.2 3.3 %copy-start.35 = (pred[128,2048]{1,0:T(8,128)(4,1)S(1)}, pred[128,2048]{1,0:T(8,128)(4,1)}, u32[]{:S(2)}) copy-start(pred[128,2048]{1,0:T(8,128)(4,1)} %get-tuple-element.24) | copy-start | bytes 786436
  173.2 3.3 %copy-start.36 = (pred[128,2048]{1,0:T(8,128)(4,1)S(1)}, pred[128,2048]{1,0:T(8,128)(4,1)}, u32[]{:S(2)}) copy-start(pred[128,2048]{1,0:T(8,128)(4,1)} %get-tuple-element.25) | copy-start | bytes 786436
  173.2 3.3 %copy-start.37 = (pred[128,2048]{1,0:T(8,128)(4,1)S(1)}, pred[128,2048]{1,0:T(8,128)(4,1)}, u32[]{:S(2)}) copy-start(pred[128,2048]{1,0:T(8,128)(4,1)} %get-tuple-element.26) | copy-start | bytes 786436
  173.2 3.3 %copy-start.38 = (pred[128,2048]{1,0:T(8,128)(4,1)S(1)}, pred[128,2048]{1,0:T(8,128)(4,1)}, u32[]{:S(2)}) copy-start(pred[128,2048]{1,0:T(8,128)(4,1)} %get-tuple-element.27) | copy-start | bytes 786436
  173.2 3.3 %copy-start.39 = (pred[128,2048]{1,0:T(8,128)(4,1)S(1)}, pred[128,2048]{1,0:T(8,128)(4,1)}, u32[]{:S(2)}) copy-start(pred[128,2048]{1,0:T(8,128)(4,1)} %get-tuple-element.28) | copy-start | bytes 786436
  173.2 3.3 %copy-start.40 = (pred[128,2048]{1,0:T(8,128)(4,1)S(1)}, pred[128,2048]{1,0:T(8,128)(4,1)}, u32[]{:S(2)}) copy-start(pred[128,2048]{1,0:T(8,128)(4,1)} %get-tuple-element.29) | copy-start | bytes 786436
  176.4 2.0 copy-start.23
  178.5 6.9 %copy-start.24 = (f32[128,2048]{1,0:T(8,128)S(1)}, f32[128,2048]{1,0:T(8,128)}, u32[]{:S(2)}) copy-start(f32[128,2048]{1,0:T(8,128)} %copy-done.23) | copy-start | bytes 3145732
  (14 other events, 13.4 us)
Sparse Core Ops, SparseCore 0:
  131.4 146.5 all-reduce.14
where the time goes:
time: 287 us; the launch traced here: 286 us
  waiting for transfers between devices  72.5 us (25%)
  blocking collectives  63 us (22%)
  local copies, waits for them, and re-layouts  61 us (21%)
  other arithmetic  45.5 us (16%)
  starting transfers between devices  27.1 us (9%)
  between operations  14.8 us (5%)
    psum x1, blocking collectives, per_device(): lax.psum((local_mat, local_cond), ('bundle', 'elem'))  63 us
    all_to_all x1, waiting for transfers between devices, return_grads(): lax.all_to_all(back_buf.reshape(n_bundle * n_elem, capacity, width), ('bu...  28.5 us
    psum x1, waiting for transfers between devices, per_device(): lax.psum((local_mat, local_cond), ('bundle', 'elem'))  26.3 us
    scatter-add x1, other arithmetic, per_device(): jax.ops.segment_sum(got_buf.astype(jnp.float32), got_ids, num_segments=el...  22.6 us
    all_to_all x1, waiting for transfers between devices, send_tiles(): lax.all_to_all(send_buf.reshape(n_bundle * n_elem, capacity, width), ('bu...  17.7 us
    gather x1, local copies, waits for them, and re-layouts, per_device(): back_buf = gsum_ext[got_ids]  14.1 us
    all_to_all x1, starting transfers between devices, send_tiles(): lax.all_to_all(send_ids.reshape(n_bundle * n_elem, capacity), ('bundle',...  11.5 us
    all_to_all x1, starting transfers between devices, send_tiles(): lax.all_to_all(send_buf.reshape(n_bundle * n_elem, capacity, width), ('bu...  9.77 us
  transfers between devices with their start and end apart: 4, of which 3 were waited for; matrix products, arithmetic and copies ran while one was open for 18% of the time, Pallas kernels for 0%

commit v1 on v0

v1 whole, which is shorter than its diff:
```python
import jax
import jax.numpy as jnp
from jax import lax
from jax.experimental import pallas as pl
from jax.experimental.pallas import tpu as pltpu
from jax.sharding import PartitionSpec as P

SEGS = 8
STEPS = 4
LANES = 128
FIB = 128
NODES = 2048
TILES = NODES // LANES
GROUPS = FIB // 8
OWNERS = 128
CAP = 32
ROWS = 40
ELEMS = 512
AXES = ("bundle", "elem")
F32 = jnp.float32
BF16 = jnp.bfloat16
NONE = -1000.0


def iota(shape, dim):
    return lax.broadcasted_iota(jnp.int32, shape, dim)


def dot(a, b):
    return jnp.dot(a, b, preferred_element_type=F32)


def dot_nt(a, b):
    return lax.dot_general(a, b, (((1,), (1,)), ((), ())), preferred_element_type=F32)


def dot_tn(a, b):
    return lax.dot_general(a, b, (((0,), (0,)), ((), ())), preferred_element_type=F32)


def onehot(mask):
    return jnp.where(mask, 1.0, 0.0)


def cut(rows):
    return [rows[:, j * LANES : (j + 1) * LANES] for j in range(TILES)]


def laplace(v, lane):
    from_left = [pltpu.roll(x, 1, axis=1) for x in v]
    from_right = [pltpu.roll(x, LANES - 1, axis=1) for x in v]
    out = []
    for j in range(TILES):
        left = jnp.where(lane == 0, from_left[j - 1] if j else v[0], from_left[j])
        right = jnp.where(
            lane == LANES - 1, from_right[j + 1] if j < TILES - 1 else v[j], from_right[j]
        )
        out.append(left + right - 2.0 * v[j])
    return out


def half_cond(seg, table):
    c = jnp.full(seg.shape, 0.5 * table[0], F32)
    for s in range(1, SEGS):
        c = jnp.where(seg == s, 0.5 * table[s], c)
    return c


def forward_kernel(table, volt, seg, owner, elem, send, qt, act):
    lane = iota((8, LANES), 1)

    def fibers(g, carry):
        rows = pl.ds(pl.multiple_of(g * 8, 8), 8)
        v = cut(volt[rows, :])
        c = cut(half_cond(seg[rows, :], table))
        for _ in range(STEPS):
            lap = laplace(v, lane)
            v = [0.5 * (x + jnp.tanh(1.5 * x)) + k * d for x, k, d in zip(v, c, lap)]
        tiles = jnp.concatenate([jnp.tanh(x) for x in v], axis=0)
        act[pl.ds(pl.multiple_of(g * LANES, LANES), LANES), :] = tiles.astype(BF16)
        return carry

    lax.fori_loop(0, GROUPS, fibers, 0)

    sub, lan = iota((LANES, LANES), 0), iota((LANES, LANES), 1)
    number = elem[...]
    raw = jnp.concatenate([owner[...], number & 255, (number >> 8) + 1], axis=0)
    order = onehot(sub == (lan % 8) * TILES + lan // 8).astype(BF16)
    ordered = dot(raw.astype(F32).astype(BF16), order)
    before = jnp.concatenate([onehot(sub < lan), jnp.ones((LANES, LANES), F32)], axis=1)
    before = before.astype(BF16)
    sub_f = sub.astype(F32)
    place = (sub % CAP).astype(F32)
    which = (sub // CAP).astype(F32)
    count = jnp.zeros((LANES, LANES), F32)
    ids = jnp.zeros((2 * OWNERS, LANES), F32)
    for b in range(GROUPS):
        own = ordered[b : b + 1, :]
        low = ordered[GROUPS + b : GROUPS + b + 1, :]
        high = ordered[2 * GROUPS + b : 2 * GROUPS + b + 1, :]
        mine = onehot(sub_f == own)
        counted = dot(mine.astype(BF16), before)
        rank = jnp.sum(mine * (counted[:, :LANES] + count), axis=0, keepdims=True)
        count = count + counted[:, LANES:]
        at_rank = place == rank
        qt[:, b * LANES : (b + 1) * LANES] = jnp.where(at_rank, own - which, NONE).astype(BF16)
        named = jnp.concatenate([mine * low, mine * high], axis=0).astype(BF16)
        ids = ids + dot_nt(named, onehot(at_rank).astype(BF16))

    row = iota((OWNERS, 8, LANES), 1)
    low_rows = jnp.broadcast_to(ids[:OWNERS][:, None, :], row.shape)
    high_rows = jnp.broadcast_to(ids[OWNERS:][:, None, :], row.shape)
    tail = jnp.where(row == 0, low_rows, jnp.where(row == 1, high_rows, 0.0))
    send[:, CAP:, :] = tail.astype(BF16)

    def slots(m, carry):
        parts = []
        for c in range(4):
            want = jnp.full((1, 1), 16 * m + 4 * c, jnp.int32).astype(F32).astype(BF16)
            parts.append(jnp.where(qt[...] == want, BF16(1), BF16(0)))
        rows = dot(jnp.concatenate(parts, axis=0), act[...]).astype(BF16)
        send[pl.ds(16 * m, 16), :CAP, :] = rows.reshape(16, CAP, LANES)
        return carry

    lax.fori_loop(0, OWNERS // 16, slots, 0)


def residual_kernel(table, volt, seg, qt, res, q):
    lane = iota((8, LANES), 1)

    def fibers(g, carry):
        rows = pl.ds(pl.multiple_of(g * 8, 8), 8)
        v = cut(volt[rows, :])
        c = cut(half_cond(seg[rows, :], table))
        for j in range(TILES):
            res[0, rows, j * LANES : (j + 1) * LANES] = c[j]
        for k in range(STEPS):
            lap = laplace(v, lane)
            new = []
            for j in range(TILES):
                t = jnp.tanh(1.5 * v[j])
                new.append(0.5 * (v[j] + t) + c[j] * lap[j])
                cols = slice(j * LANES, (j + 1) * LANES)
                res[2 + k, rows, cols] = lap[j]
                res[2 + STEPS + k, rows, cols] = 1.25 - 0.75 * t * t
            v = new
        for j in range(TILES):
            t = jnp.tanh(v[j])
            res[1, rows, j * LANES : (j + 1) * LANES] = 1.0 - t * t
        return carry

    lax.fori_loop(0, GROUPS, fibers, 0)
    for b in range(GROUPS):
        cols = slice(b * LANES, (b + 1) * LANES)
        q[cols, :] = qt[:, cols].astype(F32).T.astype(BF16)


def split_two(x):
    high = x.astype(BF16)
    return high, (x - high.astype(F32)).astype(BF16)


def element_kernel(got, cot, material, stress, back, key_row, key_col, gsum_b):
    row = iota((OWNERS, 8, LANES), 1)
    src = iota((OWNERS, 8, LANES), 0)
    lan3 = iota((OWNERS, 8, LANES), 2)
    mine = src % 4 == lan3 // CAP
    tail = got[:, CAP:, :].astype(F32)
    low = jnp.where(mine & (row == 0), tail, 0.0).astype(BF16).reshape(OWNERS * 8, LANES)
    high = jnp.where(mine & (row == 1), tail, 0.0).astype(BF16).reshape(OWNERS * 8, LANES)
    pick = onehot(iota((32, OWNERS * 8), 1) // 32 == iota((32, OWNERS * 8), 0)).astype(BF16)
    low_q = dot(pick, low)
    high_q = dot(pick, high)
    sums = []
    col = iota((256, LANES), 0).astype(F32).astype(BF16)
    slots = got[:, :CAP, :].reshape(OWNERS * CAP, LANES)
    for h in range(2):
        keys = jnp.where(high_q == h + 1, low_q, -1.0).astype(BF16)
        hit = [jnp.where(col == keys[q : q + 1, :], BF16(1), BF16(0)) for q in range(32)]
        sums.append(dot(jnp.concatenate(hit, axis=1), slots))
    summed = jnp.concatenate(sums, axis=0).astype(BF16)
    out = jnp.tanh(dot(summed, material[...]))
    stress[...] = out
    gpre = cot[...] * (1.0 - out * out)
    g_high, g_low = split_two(gpre)
    gsum_b[...] = (dot_nt(g_high, material[...]) + dot_nt(g_low, material[...])).astype(BF16)
    local = dot_tn(summed, g_high) + dot_tn(summed, g_low)
    l_high = local.astype(BF16).astype(F32)
    l_low = local - l_high
    high_rows = jnp.broadcast_to(l_high[:, None, :], row.shape)
    low_rows = jnp.broadcast_to(l_low[:, None, :], row.shape)
    back[:, CAP:, :] = jnp.where(
        row == 0, high_rows, jnp.where(row == 1, low_rows, 0.0)
    ).astype(BF16)

    key_row[...] = jnp.concatenate([low_q, high_q], axis=0)
    diagonal = iota((LANES, LANES), 0) == iota((LANES, LANES), 1)
    weigh = jnp.where(iota((2 * LANES, LANES), 0) < LANES, 1.0, 256.0).astype(BF16)
    lane = iota((1, LANES), 1).astype(F32).astype(BF16)
    for m in range(8):
        blocks = []
        for q in range(4 * m, 4 * m + 4):
            lo = jnp.where(diagonal, key_row[q : q + 1, :], 0.0)
            hi = jnp.where(diagonal, key_row[32 + q : 33 + q, :], 0.0)
            blocks.append(jnp.concatenate([lo, hi], axis=1).astype(BF16))
        key = dot(jnp.concatenate(blocks, axis=0), weigh)
        hits = []
        for c in range(4):
            part = (key - (256.0 + 128.0 * c)).astype(BF16)
            hits.append(jnp.where(part == lane, BF16(1), BF16(0)))
        rows = dot(jnp.concatenate(hits, axis=1), gsum_b[...]).astype(BF16)
        back[16 * m : 16 * m + 16, :CAP, :] = rows.reshape(16, CAP, LANES)


def adjoint_kernel(got, q, res, seg, volt_grad, last, grads, sums):
    sums[...] = jnp.zeros(sums.shape, F32)
    lane = iota((8, LANES), 1)

    def gather(m, carry):
        rows = pl.ds(pl.multiple_of(m * 512, 512), 512)
        mine = q[rows, :]
        hits = [jnp.where(mine == BF16(4 * c), BF16(1), BF16(0)) for c in range(32)]
        slots = got[:, :CAP, :].reshape(OWNERS * CAP, LANES)
        grads[rows, :] = dot(jnp.concatenate(hits, axis=1), slots)
        return carry

    lax.fori_loop(0, 4, gather, 0)

    def fibers(g, carry):
        rows = pl.ds(pl.multiple_of(g * 8, 8), 8)
        base = pl.multiple_of(g * LANES, LANES)
        scale = cut(res[1, rows, :])
        c = cut(res[0, rows, :])
        grad = [grads[pl.ds(base + 8 * j, 8), :] * scale[j] for j in range(TILES)]
        total = [jnp.zeros((8, LANES), F32)] * TILES
        for k in reversed(range(STEPS)):
            lap = cut(res[2 + k, rows, :])
            own = cut(res[2 + STEPS + k, rows, :])
            total = [t + x * d for t, x, d in zip(total, grad, lap)]
            spread = laplace([x * y for x, y in zip(grad, c)], lane)
            grad = [x * y + z for x, y, z in zip(grad, own, spread)]
        ids = cut(seg[rows, :])
        for j in range(TILES):
            volt_grad[rows, j * LANES : (j + 1) * LANES] = grad[j]
        for s in range(SEGS):
            part = jnp.where(ids[0] == s, total[0], 0.0)
            for j in range(1, TILES):
                part = part + jnp.where(ids[j] == s, total[j], 0.0)
            sums[s * 8 : s * 8 + 8, :] += part
        return carry

    lax.fori_loop(0, GROUPS, fibers, 0)
    mat = jnp.sum(got[:, CAP:, :].astype(F32), axis=0)
    mat = jnp.sum(mat[:2, :], axis=0, keepdims=True)
    lane1 = iota((1, LANES), 1)
    cond = jnp.zeros((1, LANES), F32)
    for s in range(SEGS):
        cond = jnp.where(lane1 == s, 0.5 * jnp.sum(sums[s * 8 : s * 8 + 8, :]), cond)
    both = jnp.concatenate([mat, cond], axis=0)
    last[...] = jnp.broadcast_to(both[None], last.shape)


VMEM = pl.BlockSpec(memory_space=pltpu.VMEM)
SMEM = pl.BlockSpec(memory_space=pltpu.SMEM)


def call(kernel, ins, outs, scratch, name, flops, moved, limit=48):
    return pl.pallas_call(
        kernel,
        in_specs=ins,
        out_specs=[VMEM] * len(outs),
        out_shape=[jax.ShapeDtypeStruct(s, t) for s, t in outs],
        scratch_shapes=scratch,
        compiler_params=pltpu.CompilerParams(vmem_limit_bytes=limit * 2**20),
        cost_estimate=pl.CostEstimate(flops=flops, bytes_accessed=moved, transcendentals=0),
        name=name,
    )


def exchange(x):
    return lax.all_to_all(x, AXES, split_axis=0, concat_axis=0, tiled=True)


def per_device(volt_start, seg_ids, cond_table, tile_owner, tile_elem, material, stress_cot):
    message = (OWNERS, ROWS, LANES)
    owner = tile_owner.reshape(GROUPS, LANES)
    elem = tile_elem.reshape(GROUPS, LANES)
    send, qt = call(
        forward_kernel,
        [SMEM] + [VMEM] * 4,
        [(message, BF16), ((LANES, NODES), BF16)],
        [pltpu.VMEM((NODES, LANES), BF16)],
        "forward",
        2 * 4096 * 2048 * 128,
        5 << 20,
    )(cond_table, volt_start, seg_ids, owner, elem)
    got = exchange(send)
    res, q = call(
        residual_kernel,
        [SMEM] + [VMEM] * 3,
        [((2 + 2 * STEPS, FIB, NODES), F32), ((NODES, LANES), BF16)],
        [],
        "residuals",
        1 << 28,
        14 << 20,
    )(cond_table, volt_start, seg_ids, qt)
    stress, back = call(
        element_kernel,
        [VMEM] * 3,
        [((ELEMS, LANES), F32), (message, BF16)],
        [
            pltpu.VMEM((64, LANES), F32),
            pltpu.VMEM((8, LANES), F32),
            pltpu.VMEM((ELEMS, LANES), BF16),
        ],
        "elements",
        1 << 31,
        4 << 20,
    )(got, stress_cot, material)
    got_back = exchange(back)
    volt_grad, last = call(
        adjoint_kernel,
        [VMEM] * 4,
        [((FIB, NODES), F32), ((OWNERS, 2, LANES), F32)],
        [pltpu.VMEM((NODES, LANES), F32), pltpu.VMEM((SEGS * 8, LANES), F32)],
        "adjoint",
        2 * 4096 * 2048 * 128,
        14 << 20,
    )(got_back, q, res, seg_ids)
    ends = exchange(last)
    return volt_grad, stress, ends[:, 0, :], jnp.sum(ends[:, 1, :SEGS], axis=0)


def solution(mesh):
    rows = P(AXES, None)
    return jax.shard_map(
        per_device,
        mesh=mesh,
        in_specs=(rows, rows, P(), rows, P(AXES), P(), rows),
        out_specs=(rows, rows, P(), P()),
        check_vma=False,
    )
```

time: 287 us -> 118 us (0.41)
  waiting for transfers between devices: 72.5 us -> 9.32 us
  local copies, waits for them, and re-layouts: 61 us -> 9.12 us
  Pallas kernels: 0 us -> 45.1 us
  other arithmetic: 45.5 us -> 0.66 us
  starting transfers between devices: 27.1 us -> 4.72 us
  blocking collectives: 63 us -> 47.6 us
  between operations: 14.8 us -> 0.74 us
    psum x1 -> x0, blocking collectives: 63 us -> none  [per_device(): lax.psum((local_mat, local_cond), ('bundle', 'elem'))]
    all_to_all x0 -> x2, blocking collectives: none -> 47.6 us  [exchange(): return lax.all_to_all(x, AXES, split_axis=0, concat_axis=0, tiled=True)]
    pallas_call x0 -> x4, Pallas kernels: none -> 45.1 us  [the longest x1 16.8 us: per_device(): call(adjoint_kernel, [VMEM] * 4, [((FIB, NODES), F32), ((OWNERS, 2, LANES...]
    all_to_all x3 -> x1, waiting for transfers between devices: 46.2 us -> 9.32 us  [exchange(): return lax.all_to_all(x, AXES, split_axis=0, concat_axis=0, tiled=True)]
    psum x1 -> x0, waiting for transfers between devices: 26.3 us -> none  [per_device(): lax.psum((local_mat, local_cond), ('bundle', 'elem'))]
    scatter-add x1 -> x0, other arithmetic: 22.6 us -> none  [per_device(): jax.ops.segment_sum(got_buf.astype(jnp.float32), got_ids, num_segments=el...]
    all_to_all x3 -> x1, starting transfers between devices: 27.1 us -> 4.72 us  [exchange(): return lax.all_to_all(x, AXES, split_axis=0, concat_axis=0, tiled=True)]
    gather x2 -> x0, local copies, waits for them, and re-layouts: 21.6 us -> none  [the longest x1 14.1 us: per_device(): back_buf = gsum_ext[got_ids]]
  transfers between devices with their start and end apart: 4 -> 1, of which waited for: 3 -> 1; matrix products, arithmetic and copies ran while one was open for 18% -> 0% of each run, Pallas kernels for 0% -> 9%
where the time goes in v1:
time: 118 us; the launch traced here: 117 us
  blocking collectives  47.6 us (40%)
  Pallas kernels  45.1 us (38%)
  waiting for transfers between devices  9.32 us (8%)
  local copies, waits for them, and re-layouts  9.12 us (8%)
  starting transfers between devices  4.72 us (4%)
    all_to_all x2, blocking collectives, exchange(): return lax.all_to_all(x, AXES, split_axis=0, concat_axis=0, tiled=True)  47.6 us
    pallas_call x1, Pallas kernels, per_device(): call(adjoint_kernel, [VMEM] * 4, [((FIB, NODES), F32), ((OWNERS, 2, LANES...  16.8 us
    pallas_call x1, Pallas kernels, per_device(): call(forward_kernel, [SMEM] + [VMEM] * 4, [(message, BF16), ((LANES, NODE...  13.6 us
    pallas_call x1, Pallas kernels, per_device(): call(residual_kernel, [SMEM] + [VMEM] * 3, [((2 + 2 * STEPS, FIB, NODES),...  11 us
    all_to_all x1, waiting for transfers between devices, exchange(): return lax.all_to_all(x, AXES, split_axis=0, concat_axis=0, tiled=True)  9.32 us
    unnamed x30, local copies, waits for them, and re-layouts  8.45 us
    all_to_all x1, starting transfers between devices, exchange(): return lax.all_to_all(x, AXES, split_axis=0, concat_axis=0, tiled=True)  4.72 us
    pallas_call x1, Pallas kernels, per_device(): call(element_kernel, [VMEM] * 3, [((ELEMS, LANES), F32), (message, BF16)]...  3.62 us
  transfers between devices with their start and end apart: 1, of which 1 were waited for; matrix products, arithmetic and copies ran while one was open for 0% of the time, Pallas kernels for 9%

profile of v1, /device:TPU:1, one launch (start us, length us, event | category | flops | bytes accessed | tf_op | source)
XLA Modules:
  0.0 117.2 jit_solution(12387309890250803719)
XLA Ops:
  0.6 0.0 copy-start
  0.6 1.2 %copy-done = s32[128,2048]{1,0:T(8,128)S(1)} copy-done((s32[128,2048]{1,0:T(8,128)S(1)}, s32[128,2048]{1,0:T(8,128)}, u32[]{:S(2)}) %copy-start) | copy-done | bytes 1048600
  1.9 0.0 copy-start.3
  1.9 1.2 %copy-done.3 = f32[128,2048]{1,0:T(8,128)S(1)} copy-done((f32[128,2048]{1,0:T(8,128)S(1)}, f32[128,2048]{1,0:T(8,128)}, u32[]{:S(2)}) %copy-start.3) | copy-done | bytes 1048600
  3.1 0.0 copy-start.9
  3.1 0.7 copy-done.9
  3.7 0.0 copy-start.13
  3.7 0.7 copy-done.13
  4.4 0.0 copy-start.14
  4.4 0.7 copy-done.14
  5.1 13.6 %forward.1 = (bf16[128,40,128]{2,1,0:T(8,128)(2,1)S(1)}, bf16[128,2048]{1,0:T(8,128)(2,1)S(1)}) custom-call(f32[8]{0:T(128)S(1)} %copy-done.9, f32[128,2048]{1,0:T(8,128)S(1)} %copy-done.3, s32[128,2048]{1,0:T(8,128)S(1)} %copy-done, s32[16,128]{1,0:T(8,128)S(1)} %bitcast.3, s32[16,128]{1,0:T(8,128)S(1)} %bitcast.4), custom_call_target="tpu_custom_call" | custom-call | flops 2147483648 | bytes 5242880 | tf_op jit(solution)/shard_map/forward/pallas_call | solution.py:288
  18.8 0.0 copy-start.7
  18.8 0.0 copy-start.11
  18.8 0.0 copy-start.12
  18.8 33.4 %all_to_all.15.got = bf16[128,40,128]{2,1,0:T(8,128)(2,1)S(1)} all-to-all(bf16[128,40,128]{2,1,0:T(8,128)(2,1)S(1)} %get-tuple-element.12), channel_id=1, replica_groups=mesh['bundle'=64,'elem'=2] {'bundle','elem'}, dimensions={0} | all-to-all | bytes 2621440 | tf_op jit(solution)/shard_map/all_to_all | solution.py:281
  52.2 0.0 copy-done.7
  52.2 0.0 copy-done.11
  52.2 0.0 copy-done.12
  52.2 3.6 %elements.1 = (f32[512,128]{1,0:T(8,128)}, bf16[128,40,128]{2,1,0:T(8,128)(2,1)S(1)}) custom-call(bf16[128,40,128]{2,1,0:T(8,128)(2,1)S(1)} %all_to_all.15.got, f32[512,128]{1,0:T(8,128)S(1)} %copy-done.11, bf16[128,128]{1,0:T(8,128)(2,1)S(1)} %copy-done.12), custom_call_target="tpu_custom_call" | custom-call | flops 2147483648 | bytes 4194304 | tf_op jit(solution)/shard_map/elements/pallas_call | solution.py:307
  55.8 0.0 copy-start.2
  55.9 1.1 copy-done.2
  56.9 0.0 copy-start.1
  56.9 0.0 copy-start.4
  56.9 0.0 copy-start.10
  56.9 4.7 %all-to-all-start.1 = ((bf16[128,40,128]{2,1,0:T(8,128)(2,1)}), bf16[128,40,128]{2,1,0:T(8,128)(2,1)S(1)}, u32[]{:S(2)}, u32[]{:S(2)}) async-start(bf16[128,40,128]{2,1,0:T(8,128)(2,1)} %copy-done.2), calls=%async_computation.1 | async-start | bytes 2621440 | tf_op jit(solution)/shard_map/all_to_all | solution.py:281
  61.6 0.0 copy-done.1
  61.7 0.0 copy-done.4
  61.7 0.0 copy-done.10
  61.7 0.0 copy-start.8
  61.7 1.0 copy-done.8
  62.7 11.0 %residuals.1 = (f32[10,128,2048]{2,1,0:T(8,128)}, bf16[2048,128]{1,0:T(8,128)(2,1)S(1)}) custom-call(f32[8]{0:T(128)S(1)} %copy-done.10, f32[128,2048]{1,0:T(8,128)S(1)} %copy-done.4, s32[128,2048]{1,0:T(8,128)S(1)} %copy-done.1, bf16[128,2048]{1,0:T(8,128)(2,1)S(1)} %copy-done.8), custom_call_target="tpu_custom_call" | custom-call | flops 268435456 | bytes 14680064 | tf_op jit(solution)/shard_map/residuals/pallas_call | solution.py:298
  73.7 0.0 copy-start.5
  73.8 0.8 copy-done.5
  74.5 9.3 %all-to-all-done.1.got = bf16[128,40,128]{2,1,0:T(8,128)(2,1)S(1)} async-done(((bf16[128,40,128]{2,1,0:T(8,128)(2,1)}), bf16[128,40,128]{2,1,0:T(8,128)(2,1)S(1)}, u32[]{:S(2)}, u32[]{:S(2)}) %all-to-all-start.1) | async-done | bytes 1310752 | tf_op jit(solution)/shard_map/all_to_all | solution.py:281
  83.9 0.0 copy-start.6
  83.9 1.0 copy-done.6
  84.9 16.8 %adjoint.1 = (f32[128,2048]{1,0:T(8,128)}, f32[128,2,128]{2,1,0:T(2,128)S(1)}) custom-call(bf16[128,40,128]{2,1,0:T(8,128)(2,1)S(1)} %all-to-all-done.1.got, bf16[2048,128]{1,0:T(8,128)(2,1)S(1)} %copy-done.6, f32[10,128,2048]{2,1,0:T(8,128)} %get-tuple-element.16.res, s32[128,2048]{1,0:T(8,128)S(1)} %copy-done.1), custom_call_target="tpu_custom_call" | custom-call | flops 2147483648 | bytes 14680064 | tf_op jit(solution)/shard_map/adjoint/pallas_call | solution.py:321
  101.7 14.2 %all_to_all.16 = f32[128,2,128]{2,1,0:T(2,128)S(1)} all-to-all(f32[128,2,128]{2,1,0:T(2,128)S(1)} %get-tuple-element.19), channel_id=1, replica_groups=mesh['bundle'=64,'elem'=2] {'bundle','elem'}, dimensions={0} | all-to-all | bytes 262144 | tf_op jit(solution)/shard_map/all_to_all | solution.py:281
  115.9 0.7 slice_reduce_fusion
  116.5 0.7 slice.8
Async XLA Ops:
  0.6 1.2 %copy-start = (s32[128,2048]{1,0:T(8,128)S(1)}, s32[128,2048]{1,0:T(8,128)}, u32[]{:S(2)}) copy-start(s32[128,2048]{1,0:T(8,128)} %seg.5) | copy-start | bytes 3145732
  1.9 1.2 %copy-start.3 = (f32[128,2048]{1,0:T(8,128)S(1)}, f32[128,2048]{1,0:T(8,128)}, u32[]{:S(2)}) copy-start(f32[128,2048]{1,0:T(8,128)} %volt.3) | copy-start | bytes 3145732
  3.1 0.7 copy-start.9
  3.7 0.7 copy-start.13
  4.4 0.7 copy-start.14
  18.8 33.4 %copy-start.7 = (bf16[128,2048]{1,0:T(8,128)(2,1)}, bf16[128,2048]{1,0:T(8,128)(2,1)S(1)}, u32[]{:S(2)}) copy-start(bf16[128,2048]{1,0:T(8,128)(2,1)S(1)} %get-tuple-element.14.qt) | copy-start | bytes 1572868
  18.8 33.4 %copy-start.11 = (f32[512,128]{1,0:T(8,128)S(1)}, f32[512,128]{1,0:T(8,128)}, u32[]{:S(2)}) copy-start(f32[512,128]{1,0:T(8,128)} %cot.1) | copy-start | bytes 786436
  18.8 33.4 %copy-start.12 = (bf16[128,128]{1,0:T(8,128)(2,1)S(1)}, bf16[128,128]{1,0:T(8,128)(2,1)}, u32[]{:S(2)}) copy-start(bf16[128,128]{1,0:T(8,128)(2,1)} %material.1) | copy-start | bytes 98308
  55.8 1.1 copy-start.2
  56.9 4.7 %copy-start.1 = (s32[128,2048]{1,0:T(8,128)S(1)}, s32[128,2048]{1,0:T(8,128)}, u32[]{:S(2)}) copy-start(s32[128,2048]{1,0:T(8,128)} %seg.5) | copy-start | bytes 3145732
  56.9 4.7 %copy-start.4 = (f32[128,2048]{1,0:T(8,128)S(1)}, f32[128,2048]{1,0:T(8,128)}, u32[]{:S(2)}) copy-start(f32[128,2048]{1,0:T(8,128)} %volt.3) | copy-start | bytes 3145732
  56.9 4.8 %copy-start.10 = (f32[8]{0:T(128)S(1)}, f32[8]{0:T(128)}, u32[]{:S(2)}) copy-start(f32[8]{0:T(128)} %table.3) | copy-start | bytes 100
  56.9 27.0 %all-to-all-start.1 = ((bf16[128,40,128]{2,1,0:T(8,128)(2,1)}), bf16[128,40,128]{2,1,0:T(8,128)(2,1)S(1)}, u32[]{:S(2)}, u32[]{:S(2)}) async-start(bf16[128,40,128]{2,1,0:T(8,128)(2,1)} %copy-done.2), calls=%async_computation.1 | async-start | bytes 2621440 | tf_op jit(solution)/shard_map/all_to_all | solution.py:281
  61.7 1.0 copy-start.8
  73.7 0.8 copy-start.5
  83.9 1.0 copy-start.6

commit v2 on v1

v2 whole, which is shorter than its diff:
```python
import jax
import jax.numpy as jnp
from jax import lax
from jax.experimental import pallas as pl
from jax.experimental.pallas import tpu as pltpu
from jax.sharding import PartitionSpec as P

SEGS = 8
STEPS = 4
LANES = 128
FIB = 128
NODES = 2048
TILES = NODES // LANES
GROUPS = FIB // 8
OWNERS = 128
CAP = 32
ROWS = 40
ELEMS = 512
AXES = ("bundle", "elem")
F32 = jnp.float32
BF16 = jnp.bfloat16
PART = 32
RAISE = 2.0**56
TINY = 1e-37


def iota(shape, dim):
    return lax.broadcasted_iota(jnp.int32, shape, dim)


def dot(a, b):
    return jnp.dot(a, b, preferred_element_type=F32)


def dot_nt(a, b):
    return lax.dot_general(a, b, (((1,), (1,)), ((), ())), preferred_element_type=F32)


def dot_tn(a, b):
    return lax.dot_general(a, b, (((0,), (0,)), ((), ())), preferred_element_type=F32)


def onehot(mask):
    return jnp.where(mask, 1.0, 0.0)


def cut(rows):
    return [rows[:, j * LANES : (j + 1) * LANES] for j in range(TILES)]


def neighbours(v, lane):
    from_left = [pltpu.roll(x, 1, axis=1) for x in v]
    from_right = [pltpu.roll(x, LANES - 1, axis=1) for x in v]
    out = []
    for j in range(TILES):
        left = jnp.where(lane == 0, from_left[j - 1] if j else v[0], from_left[j])
        right = jnp.where(
            lane == LANES - 1, from_right[j + 1] if j < TILES - 1 else v[j], from_right[j]
        )
        out.append(left + right)
    return out


def half_cond(seg, table):
    c = jnp.full(seg.shape, 0.5 * table[0], F32)
    for s in range(1, SEGS):
        c = jnp.where(seg == s, 0.5 * table[s], c)
    return c


def start_all(pairs, sems):
    copies = [pltpu.make_async_copy(a, b, sems.at[i]) for i, (a, b) in enumerate(pairs)]
    for c in copies:
        c.start()
    return copies


def columns(j):
    return slice(j * LANES, (j + 1) * LANES)


def forward_kernel(
    table_h, volt_h, seg_h, owner_h, elem_h, send, slots,
    table, volt, seg, owner, elem, act, stage, slot_s, sems, slot_sem,
):
    copies = start_all(
        [(owner_h, owner), (elem_h, elem), (table_h, table), (volt_h, volt), (seg_h, seg)], sems
    )
    stage[...] = jnp.zeros(stage.shape, F32)
    copies[0].wait()
    copies[1].wait()

    sub, lan = iota((LANES, LANES), 0), iota((LANES, LANES), 1)
    before = jnp.concatenate([onehot(sub < lan), jnp.ones((LANES, LANES), F32)], axis=1)
    before = before.astype(BF16)
    sub_f = sub.astype(F32)
    place = (sub % CAP).astype(F32)
    own_f = owner[...].astype(F32)
    low_f = (elem[...] & 255).astype(F32)
    high_f = ((elem[...] >> 8) + 1).astype(F32)
    count = jnp.zeros((LANES, LANES), F32)
    ids = jnp.zeros((2 * OWNERS, LANES), F32)
    for b in range(GROUPS):
        mine = onehot(sub_f == own_f[b : b + 1, :])
        counted = dot(mine.astype(BF16), before)
        rank = jnp.sum(mine * (counted[:, :LANES] + count), axis=0, keepdims=True)
        count = count + counted[:, LANES:]
        slots[b : b + 1, :] = (own_f[b : b + 1, :] * CAP + rank).astype(jnp.int32)
        named = [mine * low_f[b : b + 1, :], mine * high_f[b : b + 1, :]]
        named = jnp.concatenate(named, axis=0).astype(BF16)
        ids = ids + dot_nt(named, onehot(place == rank).astype(BF16))
    slot_copy = pltpu.make_async_copy(slots, slot_s, slot_sem)
    slot_copy.start()

    row = iota((OWNERS, 8, LANES), 1)
    low_rows = jnp.broadcast_to(ids[:OWNERS][:, None, :], row.shape)
    high_rows = jnp.broadcast_to(ids[OWNERS:][:, None, :], row.shape)
    tail = jnp.where(row == 0, low_rows, jnp.where(row == 1, high_rows, 0.0))
    send[:, CAP:, :] = tail.astype(BF16)
    for c in copies[2:]:
        c.wait()

    lane = iota((PART, LANES), 1)

    def fibers(g):
        rows = slice(g * PART, (g + 1) * PART)
        v = [1.5 * x for x in cut(volt[rows, :])]
        c = cut(half_cond(seg[rows, :], table))
        own = [0.5 - 2.0 * x for x in c]
        for _ in range(STEPS):
            both = neighbours(v, lane)
            v = [
                x * a + 0.75 * jnp.tanh(x) + k * y for x, a, k, y in zip(v, own, c, both)
            ]
        for j in range(TILES):
            act[rows, columns(j)] = jnp.tanh(v[j] * (1.0 / 1.5))

    def scatter(g):
        for f in range(g * PART, (g + 1) * PART):
            for j in range(TILES):
                slot = slot_s[f // 8, f % 8 * TILES + j]
                stage[pl.ds(slot, 1), :] = act[f : f + 1, columns(j)]

    fibers(0)
    slot_copy.wait()
    for g in range(1, FIB // PART):
        scatter(g - 1)
        fibers(g)
    scatter(FIB // PART - 1)
    for m in range(8):
        rows = stage[512 * m : 512 * (m + 1), :].astype(BF16)
        send[16 * m : 16 * (m + 1), :CAP, :] = rows.reshape(16, CAP, LANES)


def residual_kernel(table_h, volt_h, seg_h, res, table, volt, seg, sems):
    for c in start_all([(table_h, table), (volt_h, volt), (seg_h, seg)], sems):
        c.wait()
    lane = iota((PART, LANES), 1)

    def fibers(g, carry):
        rows = pl.ds(pl.multiple_of(g * PART, PART), PART)
        v = cut(volt[rows, :])
        c = cut(half_cond(seg[rows, :], table))
        for j in range(TILES):
            res[0, rows, columns(j)] = c[j]
        for k in range(STEPS):
            both = neighbours(v, lane)
            new = []
            for j in range(TILES):
                t = jnp.tanh(1.5 * v[j])
                lap = both[j] - 2.0 * v[j]
                new.append(0.5 * (v[j] + t) + c[j] * lap)
                res[2 + k, rows, columns(j)] = lap
                res[2 + STEPS + k, rows, columns(j)] = 1.25 - 0.75 * t * t - 2.0 * c[j]
            v = new
        for j in range(TILES):
            t = jnp.tanh(v[j])
            res[1, rows, columns(j)] = (1.0 - t * t) * (1.0 / RAISE)
        return carry

    lax.fori_loop(0, FIB // PART, fibers, 0)


def split_two(x):
    high = x.astype(BF16)
    return high, (x - high.astype(F32)).astype(BF16)


def element_kernel(got, cot, material, stress, back, key_row, key_col, gsum_b):
    row = iota((OWNERS, 8, LANES), 1)
    src = iota((OWNERS, 8, LANES), 0)
    lan3 = iota((OWNERS, 8, LANES), 2)
    mine = src % 4 == lan3 // CAP
    tail = got[:, CAP:, :].astype(F32)
    low = jnp.where(mine & (row == 0), tail, 0.0).astype(BF16).reshape(OWNERS * 8, LANES)
    high = jnp.where(mine & (row == 1), tail, 0.0).astype(BF16).reshape(OWNERS * 8, LANES)
    pick = onehot(iota((32, OWNERS * 8), 1) // 32 == iota((32, OWNERS * 8), 0)).astype(BF16)
    low_q = dot(pick, low)
    high_q = dot(pick, high)
    sums = []
    col = iota((256, LANES), 0).astype(F32).astype(BF16)
    slots = got[:, :CAP, :].reshape(OWNERS * CAP, LANES)
    for h in range(2):
        keys = jnp.where(high_q == h + 1, low_q, -1.0).astype(BF16)
        hit = [jnp.where(col == keys[q : q + 1, :], BF16(1), BF16(0)) for q in range(32)]
        sums.append(dot(jnp.concatenate(hit, axis=1), slots))
    summed = jnp.concatenate(sums, axis=0).astype(BF16)
    out = jnp.tanh(dot(summed, material[...]))
    stress[...] = out
    gpre = cot[...] * (1.0 - out * out)
    g_high, g_low = split_two(gpre)
    raised = (dot_nt(g_high, material[...]) + dot_nt(g_low, material[...])) * RAISE
    gsum_b[...] = (raised * jnp.abs(raised)).astype(BF16)
    local = dot_tn(summed, g_high) + dot_tn(summed, g_low)
    l_high = local.astype(BF16).astype(F32)
    l_low = local - l_high
    high_rows = jnp.broadcast_to(l_high[:, None, :], row.shape)
    low_rows = jnp.broadcast_to(l_low[:, None, :], row.shape)
    back[:, CAP:, :] = jnp.where(
        row == 0, high_rows, jnp.where(row == 1, low_rows, 0.0)
    ).astype(BF16)

    key_row[...] = jnp.concatenate([low_q, high_q], axis=0)
    diagonal = iota((LANES, LANES), 0) == iota((LANES, LANES), 1)
    weigh = jnp.where(iota((2 * LANES, LANES), 0) < LANES, 1.0, 256.0).astype(BF16)
    lane = iota((1, LANES), 1).astype(F32).astype(BF16)
    for m in range(8):
        blocks = []
        for q in range(4 * m, 4 * m + 4):
            lo = jnp.where(diagonal, key_row[q : q + 1, :], 0.0)
            hi = jnp.where(diagonal, key_row[32 + q : 33 + q, :], 0.0)
            blocks.append(jnp.concatenate([lo, hi], axis=1).astype(BF16))
        key = dot(jnp.concatenate(blocks, axis=0), weigh)
        hits = []
        for c in range(4):
            part = (key - (256.0 + 128.0 * c)).astype(BF16)
            hits.append(jnp.where(part == lane, BF16(1), BF16(0)))
        rows = dot(jnp.concatenate(hits, axis=1), gsum_b[...]).astype(BF16)
        back[16 * m : 16 * m + 16, :CAP, :] = rows.reshape(16, CAP, LANES)


def adjoint_kernel(
    got, slots_h, res, seg_h, volt_grad, last, rows_s, grads, sums, slot_s, seg, sems
):
    copies = start_all([(slots_h, slot_s), (seg_h, seg)], sems)
    for m in range(8):
        rows = got[16 * m : 16 * (m + 1), :CAP, :].astype(F32)
        rows_s[512 * m : 512 * (m + 1), :] = rows.reshape(512, LANES)
    for c in copies:
        c.wait()
    lane = iota((PART, LANES), 1)

    def gather(g):
        for f in range(g * PART, (g + 1) * PART):
            for j in range(TILES):
                slot = slot_s[f // 8, f % 8 * TILES + j]
                grads[f : f + 1, columns(j)] = rows_s[pl.ds(slot, 1), :]

    def fibers(g):
        rows = slice(g * PART, (g + 1) * PART)
        coded = cut(grads[rows, :])
        c = cut(res[0, rows, :])
        scale = cut(res[1, rows, :])
        grad = [
            x * lax.rsqrt(jnp.maximum(jnp.abs(x), TINY)) * y for x, y in zip(coded, scale)
        ]
        total = [jnp.zeros((PART, LANES), F32)] * TILES
        for k in reversed(range(STEPS)):
            lap = cut(res[2 + k, rows, :])
            own = cut(res[2 + STEPS + k, rows, :])
            total = [t + x * d for t, x, d in zip(total, grad, lap)]
            both = neighbours([x * y for x, y in zip(grad, c)], lane)
            grad = [x * y + z for x, y, z in zip(grad, own, both)]
        ids = cut(seg[rows, :])
        for j in range(TILES):
            volt_grad[rows, columns(j)] = grad[j]
        for s in range(SEGS):
            part = jnp.where(ids[0] == s, total[0], 0.0)
            for j in range(1, TILES):
                part = part + jnp.where(ids[j] == s, total[j], 0.0)
            part = jnp.sum(part.reshape(PART // 8, 8, LANES), axis=0)
            if g:
                part = part + sums[s * 8 : s * 8 + 8, :]
            sums[s * 8 : s * 8 + 8, :] = part

    gather(0)
    for g in range(FIB // PART):
        if g + 1 < FIB // PART:
            gather(g + 1)
        fibers(g)
    mat = jnp.sum(got[:, CAP:, :].astype(F32), axis=0)
    mat = jnp.sum(mat[:2, :], axis=0, keepdims=True)
    part = jnp.sum(sums[...].reshape(SEGS, 8, LANES), axis=1)
    part = 0.5 * jnp.sum(part, axis=1, keepdims=True)
    spot = iota((SEGS, LANES), 0) == iota((SEGS, LANES), 1)
    cond = jnp.sum(jnp.where(spot, part, 0.0), axis=0, keepdims=True)
    both = jnp.concatenate([mat, cond], axis=0)
    last[...] = jnp.broadcast_to(both[None], last.shape)


VMEM = pl.BlockSpec(memory_space=pltpu.VMEM)
HBM = pl.BlockSpec(memory_space=pltpu.HBM)


def call(kernel, ins, outs, scratch, name, flops, moved, limit=48):
    return pl.pallas_call(
        kernel,
        in_specs=ins,
        out_specs=[VMEM] * len(outs),
        out_shape=[jax.ShapeDtypeStruct(s, t) for s, t in outs],
        scratch_shapes=scratch,
        compiler_params=pltpu.CompilerParams(vmem_limit_bytes=limit * 2**20),
        cost_estimate=pl.CostEstimate(flops=flops, bytes_accessed=moved, transcendentals=0),
        name=name,
    )


def exchange(x):
    return lax.all_to_all(x, AXES, split_axis=0, concat_axis=0, tiled=True)


def per_device(volt_start, seg_ids, cond_table, tile_owner, tile_elem, material, stress_cot):
    message = (OWNERS, ROWS, LANES)
    owner = tile_owner.reshape(GROUPS, LANES)
    elem = tile_elem.reshape(GROUPS, LANES)
    fibers = (FIB, NODES)
    index = (GROUPS, LANES)
    send, slots = call(
        forward_kernel,
        [HBM] * 5,
        [(message, BF16), (index, jnp.int32)],
        [
            pltpu.SMEM((SEGS,), F32),
            pltpu.VMEM(fibers, F32),
            pltpu.VMEM(fibers, jnp.int32),
            pltpu.VMEM(index, jnp.int32),
            pltpu.VMEM(index, jnp.int32),
            pltpu.VMEM(fibers, F32),
            pltpu.VMEM((OWNERS * CAP, LANES), F32),
            pltpu.SMEM(index, jnp.int32),
            pltpu.SemaphoreType.DMA((5,)),
            pltpu.SemaphoreType.DMA,
        ],
        "forward",
        1 << 28,
        5 << 20,
    )(cond_table, volt_start, seg_ids, owner, elem)
    got = exchange(send)
    res = call(
        residual_kernel,
        [HBM] * 3,
        [((2 + 2 * STEPS, FIB, NODES), F32)],
        [
            pltpu.SMEM((SEGS,), F32),
            pltpu.VMEM(fibers, F32),
            pltpu.VMEM(fibers, jnp.int32),
            pltpu.SemaphoreType.DMA((3,)),
        ],
        "residuals",
        1 << 28,
        14 << 20,
    )(cond_table, volt_start, seg_ids)[0]
    stress, back = call(
        element_kernel,
        [VMEM] * 3,
        [((ELEMS, LANES), F32), (message, BF16)],
        [
            pltpu.VMEM((64, LANES), F32),
            pltpu.VMEM((8, LANES), F32),
            pltpu.VMEM((ELEMS, LANES), BF16),
        ],
        "elements",
        1 << 31,
        4 << 20,
    )(got, stress_cot, material)
    got_back = exchange(back)
    volt_grad, last = call(
        adjoint_kernel,
        [VMEM, HBM, VMEM, HBM],
        [(fibers, F32), ((OWNERS, 2, LANES), F32)],
        [
            pltpu.VMEM((OWNERS * CAP, LANES), F32),
            pltpu.VMEM(fibers, F32),
            pltpu.VMEM((SEGS * 8, LANES), F32),
            pltpu.SMEM(index, jnp.int32),
            pltpu.VMEM(fibers, jnp.int32),
            pltpu.SemaphoreType.DMA((2,)),
        ],
        "adjoint",
        1 << 28,
        14 << 20,
    )(got_back, slots, res, seg_ids)
    ends = exchange(last)
    return volt_grad, stress, ends[:, 0, :], jnp.sum(ends[:, 1, :SEGS], axis=0)


def solution(mesh):
    rows = P(AXES, None)
    return jax.shard_map(
        per_device,
        mesh=mesh,
        in_specs=(rows, rows, P(), rows, P(AXES), P(), rows),
        out_specs=(rows, rows, P(), P()),
        check_vma=False,
    )
```

time: 118 us -> 102 us (0.86)
  Pallas kernels: 45.1 us -> 27.5 us
  waiting for transfers between devices: 9.32 us -> 13.9 us
  local copies, waits for them, and re-layouts: 9.12 us -> 6.25 us
    pallas_call x3, Pallas kernels: 41.4 us -> 23.9 us  [the longest x1 10.4 us: per_device(): call(adjoint_kernel, [VMEM, HBM, VMEM, HBM], [(fibers, F32), ((OWNERS, 2,...]
    all_to_all x1, waiting for transfers between devices: 9.32 us -> 13.9 us  [exchange(): return lax.all_to_all(x, AXES, split_axis=0, concat_axis=0, tiled=True)]
    unnamed x30 -> x22, local copies, waits for them, and re-layouts: 8.45 us -> 5.57 us
  transfers between devices with their start and end apart: 1 -> 1, of which waited for: 1 -> 1; matrix products, arithmetic and copies ran while one was open for 0% -> 0% of each run, Pallas kernels for 9% -> 8%
where the time goes in v2:
time: 102 us; the launch traced here: 101 us
  blocking collectives  47.6 us (47%)
  Pallas kernels  27.5 us (27%)
  waiting for transfers between devices  13.9 us (14%)
  local copies, waits for them, and re-layouts  6.25 us (6%)
  starting transfers between devices  4.74 us (5%)
    all_to_all x2, blocking collectives, exchange(): return lax.all_to_all(x, AXES, split_axis=0, concat_axis=0, tiled=True)  47.6 us
    all_to_all x1, waiting for transfers between devices, exchange(): return lax.all_to_all(x, AXES, split_axis=0, concat_axis=0, tiled=True)  13.9 us
    pallas_call x1, Pallas kernels, per_device(): call(adjoint_kernel, [VMEM, HBM, VMEM, HBM], [(fibers, F32), ((OWNERS, 2,...  10.4 us
    pallas_call x1, Pallas kernels, per_device(): call(residual_kernel, [HBM] * 3, [((2 + 2 * STEPS, FIB, NODES), F32)], [p...  8.28 us
    unnamed x22, local copies, waits for them, and re-layouts  5.57 us
    pallas_call x1, Pallas kernels, per_device(): call(forward_kernel, [HBM] * 5, [(message, BF16), (index, jnp.int32)], [p...  5.18 us
    all_to_all x1, starting transfers between devices, exchange(): return lax.all_to_all(x, AXES, split_axis=0, concat_axis=0, tiled=True)  4.74 us
    pallas_call x1, Pallas kernels, per_device(): call(element_kernel, [VMEM] * 3, [((ELEMS, LANES), F32), (message, BF16)]...  3.62 us
  transfers between devices with their start and end apart: 1, of which 1 were waited for; matrix products, arithmetic and copies ran while one was open for 0% of the time, Pallas kernels for 8%

profile of v2, /device:TPU:1, one launch (start us, length us, event | category | flops | bytes accessed | tf_op | source)
XLA Modules:
  0.0 101.3 jit_solution(15297724998355207921)
XLA Ops:
  0.6 0.0 copy-start
  0.6 1.2 %copy-done = s32[128,2048]{1,0:T(8,128)S(1)} copy-done((s32[128,2048]{1,0:T(8,128)S(1)}, s32[128,2048]{1,0:T(8,128)}, u32[]{:S(2)}) %copy-start) | copy-done | bytes 1048600
  1.9 0.0 copy-start.2
  1.9 1.2 %copy-done.2 = f32[128,2048]{1,0:T(8,128)S(1)} copy-done((f32[128,2048]{1,0:T(8,128)S(1)}, f32[128,2048]{1,0:T(8,128)}, u32[]{:S(2)}) %copy-start.2) | copy-done | bytes 1048600
  3.1 0.0 copy-start.5
  3.1 0.7 copy-done.5
  3.8 0.0 copy-start.6
  3.8 0.7 copy-done.6
  4.5 0.0 copy-start.7
  4.5 0.7 copy-done.7
  5.1 5.2 %forward.1 = (bf16[128,40,128]{2,1,0:T(8,128)(2,1)S(1)}, s32[16,128]{1,0:T(8,128)S(1)}) custom-call(f32[8]{0:T(128)S(1)} %copy-done.7, f32[128,2048]{1,0:T(8,128)S(1)} %copy-done.2, s32[128,2048]{1,0:T(8,128)S(1)} %copy-done, s32[16,128]{1,0:T(8,128)S(1)} %bitcast.3, s32[16,128]{1,0:T(8,128)S(1)} %bitcast.4), custom_call_target="tpu_custom_call" | custom-call | flops 268435456 | bytes 5242880 | tf_op jit(solution)/shard_map/forward/pallas_call | solution.py:328
  10.3 0.0 copy-start.9
  10.3 0.0 copy-start.10
  10.3 33.4 %all_to_all.15.got = bf16[128,40,128]{2,1,0:T(8,128)(2,1)S(1)} all-to-all(bf16[128,40,128]{2,1,0:T(8,128)(2,1)S(1)} %get-tuple-element.10), channel_id=1, replica_groups=mesh['bundle'=64,'elem'=2] {'bundle','elem'}, dimensions={0} | all-to-all | bytes 2621440 | tf_op jit(solution)/shard_map/all_to_all | solution.py:319
  43.7 0.0 copy-done.9
  43.7 0.0 copy-done.10
  43.7 3.6 %elements.1 = (f32[512,128]{1,0:T(8,128)}, bf16[128,40,128]{2,1,0:T(8,128)(2,1)S(1)}) custom-call(bf16[128,40,128]{2,1,0:T(8,128)(2,1)S(1)} %all_to_all.15.got, f32[512,128]{1,0:T(8,128)S(1)} %copy-done.9, bf16[128,128]{1,0:T(8,128)(2,1)S(1)} %copy-done.10), custom_call_target="tpu_custom_call" | custom-call | flops 2147483648 | bytes 4194304 | tf_op jit(solution)/shard_map/elements/pallas_call | solution.py:363
  47.4 0.0 copy-start.4
  47.4 1.1 %copy-done.4 = bf16[128,40,128]{2,1,0:T(8,128)(2,1)} copy-done((bf16[128,40,128]{2,1,0:T(8,128)(2,1)}, bf16[128,40,128]{2,1,0:T(8,128)(2,1)S(1)}, u32[]{:S(2)}) %copy-start.4) | copy-done | bytes 1310744
  48.4 0.0 copy-start.1
  48.4 0.0 copy-start.3
  48.4 0.0 copy-start.8
  48.4 4.7 %all-to-all-start.1 = ((bf16[128,40,128]{2,1,0:T(8,128)(2,1)}), bf16[128,40,128]{2,1,0:T(8,128)(2,1)S(1)}, u32[]{:S(2)}, u32[]{:S(2)}) async-start(bf16[128,40,128]{2,1,0:T(8,128)(2,1)} %copy-done.4), calls=%async_computation.1 | async-start | bytes 2621440 | tf_op jit(solution)/shard_map/all_to_all | solution.py:319
  53.2 0.0 copy-done.1
  53.2 0.0 copy-done.3
  53.2 0.0 copy-done.8
  53.2 8.3 %residuals.1.res = f32[10,128,2048]{2,1,0:T(8,128)} custom-call(f32[8]{0:T(128)S(1)} %copy-done.8, f32[128,2048]{1,0:T(8,128)S(1)} %copy-done.3, s32[128,2048]{1,0:T(8,128)S(1)} %copy-done.1), custom_call_target="tpu_custom_call" | custom-call | flops 268435456 | bytes 14680064 | tf_op jit(solution)/shard_map/residuals/pallas_call | solution.py:349
  61.5 13.9 %all-to-all-done.1.got = bf16[128,40,128]{2,1,0:T(8,128)(2,1)S(1)} async-done(((bf16[128,40,128]{2,1,0:T(8,128)(2,1)}), bf16[128,40,128]{2,1,0:T(8,128)(2,1)S(1)}, u32[]{:S(2)}, u32[]{:S(2)}) %all-to-all-start.1) | async-done | bytes 1310752 | tf_op jit(solution)/shard_map/all_to_all | solution.py:319
  75.4 10.4 %adjoint.1 = (f32[128,2048]{1,0:T(8,128)}, f32[128,2,128]{2,1,0:T(2,128)S(1)}) custom-call(bf16[128,40,128]{2,1,0:T(8,128)(2,1)S(1)} %all-to-all-done.1.got, s32[16,128]{1,0:T(8,128)S(1)} %get-tuple-element.12.slots_h, f32[10,128,2048]{2,1,0:T(8,128)} %residuals.1.res, s32[128,2048]{1,0:T(8,128)S(1)} %copy-done.1), custom_call_target="tpu_custom_call" | custom-call | flops 268435456 | bytes 14680064 | tf_op jit(solution)/shard_map/adjoint/pallas_call | solution.py:377
  85.8 14.2 %all_to_all.16 = f32[128,2,128]{2,1,0:T(2,128)S(1)} all-to-all(f32[128,2,128]{2,1,0:T(2,128)S(1)} %get-tuple-element.15), channel_id=1, replica_groups=mesh['bundle'=64,'elem'=2] {'bundle','elem'}, dimensions={0} | all-to-all | bytes 262144 | tf_op jit(solution)/shard_map/all_to_all | solution.py:319
  100.0 0.7 slice_reduce_fusion
  100.7 0.7 slice.8
Async XLA Ops:
  0.6 1.2 %copy-start = (s32[128,2048]{1,0:T(8,128)S(1)}, s32[128,2048]{1,0:T(8,128)}, u32[]{:S(2)}) copy-start(s32[128,2048]{1,0:T(8,128)} %seg_h.5) | copy-start | bytes 3145732
  1.9 1.2 %copy-start.2 = (f32[128,2048]{1,0:T(8,128)S(1)}, f32[128,2048]{1,0:T(8,128)}, u32[]{:S(2)}) copy-start(f32[128,2048]{1,0:T(8,128)} %volt_h.3) | copy-start | bytes 3145732
  3.1 0.7 copy-start.5
  3.8 0.7 copy-start.6
  4.5 0.7 copy-start.7
  10.3 33.4 %copy-start.9 = (f32[512,128]{1,0:T(8,128)S(1)}, f32[512,128]{1,0:T(8,128)}, u32[]{:S(2)}) copy-start(f32[512,128]{1,0:T(8,128)} %cot.1) | copy-start | bytes 786436
  10.3 33.4 %copy-start.10 = (bf16[128,128]{1,0:T(8,128)(2,1)S(1)}, bf16[128,128]{1,0:T(8,128)(2,1)}, u32[]{:S(2)}) copy-start(bf16[128,128]{1,0:T(8,128)(2,1)} %material.1) | copy-start | bytes 98308
  47.4 1.1 %copy-start.4 = (bf16[128,40,128]{2,1,0:T(8,128)(2,1)}, bf16[128,40,128]{2,1,0:T(8,128)(2,1)S(1)}, u32[]{:S(2)}) copy-start(bf16[128,40,128]{2,1,0:T(8,128)(2,1)S(1)} %get-tuple-element.11) | copy-start | bytes 3932164
  48.4 4.8 %copy-start.1 = (s32[128,2048]{1,0:T(8,128)S(1)}, s32[128,2048]{1,0:T(8,128)}, u32[]{:S(2)}) copy-start(s32[128,2048]{1,0:T(8,128)} %seg_h.5) | copy-start | bytes 3145732
  48.4 4.8 %copy-start.3 = (f32[128,2048]{1,0:T(8,128)S(1)}, f32[128,2048]{1,0:T(8,128)}, u32[]{:S(2)}) copy-start(f32[128,2048]{1,0:T(8,128)} %volt_h.3) | copy-start | bytes 3145732
  48.4 4.8 %copy-start.8 = (f32[8]{0:T(128)S(1)}, f32[8]{0:T(128)}, u32[]{:S(2)}) copy-start(f32[8]{0:T(128)} %table_h.3) | copy-start | bytes 100
  48.4 27.0 %all-to-all-start.1 = ((bf16[128,40,128]{2,1,0:T(8,128)(2,1)}), bf16[128,40,128]{2,1,0:T(8,128)(2,1)S(1)}, u32[]{:S(2)}, u32[]{:S(2)}) async-start(bf16[128,40,128]{2,1,0:T(8,128)(2,1)} %copy-done.4), calls=%async_computation.1 | async-start | bytes 2621440 | tf_op jit(solution)/shard_map/all_to_all | solution.py:319

commit v3 on v2

--- a/solution.py
+++ b/solution.py
@@ -20,6 +20,7 @@
 F32 = jnp.float32
 BF16 = jnp.bfloat16
 PART = 32
+CHUNKS = 4
 RAISE = 2.0**56
 TINY = 1e-37
 
@@ -147,9 +148,11 @@
         scatter(g - 1)
         fibers(g)
     scatter(FIB // PART - 1)
-    for m in range(8):
-        rows = stage[512 * m : 512 * (m + 1), :].astype(BF16)
-        send[16 * m : 16 * (m + 1), :CAP, :] = rows.reshape(16, CAP, LANES)
+    leave = []
+    for m in range(CHUNKS):
+        some = slice(m * OWNERS // CHUNKS, (m + 1) * OWNERS // CHUNKS)
+        rows = stage[CAP * some.start : CAP * some.stop, :].astype(BF16)
+        send[some, :CAP, :] = rows.reshape(-1, CAP, LANES)
 
 
 def residual_kernel(table_h, volt_h, seg_h, res, table, volt, seg, sems):
@@ -186,7 +189,7 @@
     return high, (x - high.astype(F32)).astype(BF16)
 
 
-def element_kernel(got, cot, material, stress, back, key_row, key_col, gsum_b):
+def element_kernel(got, cot, material, stress, back, key_row, gsum_b):
     row = iota((OWNERS, 8, LANES), 1)
     src = iota((OWNERS, 8, LANES), 0)
     lan3 = iota((OWNERS, 8, LANES), 2)
@@ -224,6 +227,7 @@
     diagonal = iota((LANES, LANES), 0) == iota((LANES, LANES), 1)
     weigh = jnp.where(iota((2 * LANES, LANES), 0) < LANES, 1.0, 256.0).astype(BF16)
     lane = iota((1, LANES), 1).astype(F32).astype(BF16)
+    leave = []
     for m in range(8):
         blocks = []
         for q in range(4 * m, 4 * m + 4):
@@ -236,13 +240,17 @@
             part = (key - (256.0 + 128.0 * c)).astype(BF16)
             hits.append(jnp.where(part == lane, BF16(1), BF16(0)))
         rows = dot(jnp.concatenate(hits, axis=1), gsum_b[...]).astype(BF16)
-        back[16 * m : 16 * m + 16, :CAP, :] = rows.reshape(16, CAP, LANES)
+        some = slice(16 * m, 16 * m + 16)
+        back[some, :CAP, :] = rows.reshape(16, CAP, LANES)
 
 
 def adjoint_kernel(
-    got, slots_h, res, seg_h, volt_grad, last, rows_s, grads, sums, slot_s, seg, sems
+    got, slots_h, res_h, seg_h, volt_h, last,
+    rows_s, grads, sums, slot_s, seg, res, volt_grad, sems, res_sems, out_sems,
 ):
     copies = start_all([(slots_h, slot_s), (seg_h, seg)], sems)
+    parts = [slice(g * PART, (g + 1) * PART) for g in range(FIB // PART)]
+    arrive = start_all([(res_h.at[:, p, :], res.at[:, p, :]) for p in parts], res_sems)
     for m in range(8):
         rows = got[16 * m : 16 * (m + 1), :CAP, :].astype(F32)
         rows_s[512 * m : 512 * (m + 1), :] = rows.reshape(512, LANES)
@@ -284,10 +292,13 @@
             sums[s * 8 : s * 8 + 8, :] = part
 
     gather(0)
-    for g in range(FIB // PART):
+    leave = []
+    for g, p in enumerate(parts):
+        arrive[g].wait()
         if g + 1 < FIB // PART:
             gather(g + 1)
         fibers(g)
+        leave += start_all([(volt_grad.at[p], volt_h.at[p])], out_sems.at[g : g + 1])
     mat = jnp.sum(got[:, CAP:, :].astype(F32), axis=0)
     mat = jnp.sum(mat[:2, :], axis=0, keepdims=True)
     part = jnp.sum(sums[...].reshape(SEGS, 8, LANES), axis=1)
@@ -296,17 +307,25 @@
     cond = jnp.sum(jnp.where(spot, part, 0.0), axis=0, keepdims=True)
     both = jnp.concatenate([mat, cond], axis=0)
     last[...] = jnp.broadcast_to(both[None], last.shape)
+    for c in leave:
+        c.wait()
+
+
+def last_kernel(ends, material_grad, cond_grad):
+    both = ends[...]
+    material_grad[...] = both[:, 0, :]
+    cond_grad[...] = jnp.sum(both, axis=0)[1, :SEGS]
 
 
 VMEM = pl.BlockSpec(memory_space=pltpu.VMEM)
 HBM = pl.BlockSpec(memory_space=pltpu.HBM)
 
 
-def call(kernel, ins, outs, scratch, name, flops, moved, limit=48):
+def call(kernel, ins, outs, scratch, name, flops, moved, limit=48, where=None):
     return pl.pallas_call(
         kernel,
         in_specs=ins,
-        out_specs=[VMEM] * len(outs),
+        out_specs=where or [VMEM] * len(outs),
         out_shape=[jax.ShapeDtypeStruct(s, t) for s, t in outs],
         scratch_shapes=scratch,
         compiler_params=pltpu.CompilerParams(vmem_limit_bytes=limit * 2**20),
@@ -344,6 +363,8 @@
         "forward",
         1 << 28,
         5 << 20,
+        60,
+        [VMEM, VMEM],
     )(cond_table, volt_start, seg_ids, owner, elem)
     got = exchange(send)
     res = call(
@@ -366,17 +387,18 @@
         [((ELEMS, LANES), F32), (message, BF16)],
         [
             pltpu.VMEM((64, LANES), F32),
-            pltpu.VMEM((8, LANES), F32),
             pltpu.VMEM((ELEMS, LANES), BF16),
         ],
         "elements",
         1 << 31,
         4 << 20,
+        32,
+        [VMEM, VMEM],
     )(got, stress_cot, material)
     got_back = exchange(back)
     volt_grad, last = call(
         adjoint_kernel,
-        [VMEM, HBM, VMEM, HBM],
+        [VMEM, HBM, HBM, HBM],
         [(fibers, F32), ((OWNERS, 2, LANES), F32)],
         [
             pltpu.VMEM((OWNERS * CAP, LANES), F32),
@@ -384,14 +406,29 @@
             pltpu.VMEM((SEGS * 8, LANES), F32),
             pltpu.SMEM(index, jnp.int32),
             pltpu.VMEM(fibers, jnp.int32),
+            pltpu.VMEM((2 + 2 * STEPS, *fibers), F32),
+            pltpu.VMEM(fibers, F32),
             pltpu.SemaphoreType.DMA((2,)),
+            pltpu.SemaphoreType.DMA((FIB // PART,)),
+            pltpu.SemaphoreType.DMA((FIB // PART,)),
         ],
         "adjoint",
         1 << 28,
         14 << 20,
+        48,
+        [HBM, VMEM],
     )(got_back, slots, res, seg_ids)
     ends = exchange(last)
-    return volt_grad, stress, ends[:, 0, :], jnp.sum(ends[:, 1, :SEGS], axis=0)
+    material_grad, cond_grad = call(
+        last_kernel,
+        [VMEM],
+        [((LANES, LANES), F32), ((SEGS,), F32)],
+        [],
+        "last_sums",
+        1 << 16,
+        1 << 17,
+    )(ends)
+    return volt_grad, stress, material_grad, cond_grad
 
 
 def solution(mesh):

time: 102 us -> 94.7 us (0.928)
  local copies, waits for them, and re-layouts: 6.25 us -> 1.1 us
  Pallas kernels: 27.5 us -> 26.1 us
    unnamed x22 -> x14, local copies, waits for them, and re-layouts: 5.57 us -> 1.1 us
    pallas_call x1 -> x2, Pallas kernels: 10.4 us -> 7.63 us  [the longest x1 6.94 us: per_device(): call(adjoint_kernel, [VMEM, HBM, HBM, HBM], [(fibers, F32), ((OWNERS, 2,...]
    pallas_call x1, Pallas kernels: 5.18 us -> 6.6 us  [per_device(): call(forward_kernel, [HBM] * 5, [(message, BF16), (index, jnp.int32)], [p...]
  transfers between devices with their start and end apart: 1 -> 1, of which waited for: 1 -> 1; matrix products, arithmetic and copies ran while one was open for 0% -> 0% of each run, Pallas kernels for 8% -> 9%
where the time goes in v3:
time: 94.7 us; the launch traced here: 94.4 us
  blocking collectives  47.8 us (50%)
  Pallas kernels  26.1 us (28%)
  waiting for transfers between devices  13.9 us (15%)
  starting transfers between devices  4.73 us (5%)
  local copies, waits for them, and re-layouts  1.1 us (1%)
    all_to_all x2, blocking collectives, exchange(): return lax.all_to_all(x, AXES, split_axis=0, concat_axis=0, tiled=True)  47.8 us
    all_to_all x1, waiting for transfers between devices, exchange(): return lax.all_to_all(x, AXES, split_axis=0, concat_axis=0, tiled=True)  13.9 us
    pallas_call x1, Pallas kernels, per_device(): call(residual_kernel, [HBM] * 3, [((2 + 2 * STEPS, FIB, NODES), F32)], [p...  8.28 us
    pallas_call x1, Pallas kernels, per_device(): call(adjoint_kernel, [VMEM, HBM, HBM, HBM], [(fibers, F32), ((OWNERS, 2,...  6.94 us
    pallas_call x1, Pallas kernels, per_device(): call(forward_kernel, [HBM] * 5, [(message, BF16), (index, jnp.int32)], [p...  6.6 us
    all_to_all x1, starting transfers between devices, exchange(): return lax.all_to_all(x, AXES, split_axis=0, concat_axis=0, tiled=True)  4.73 us
    pallas_call x1, Pallas kernels, per_device(): call(element_kernel, [VMEM] * 3, [((ELEMS, LANES), F32), (message, BF16)]...  3.63 us
  transfers between devices with their start and end apart: 1, of which 1 were waited for; matrix products, arithmetic and copies ran while one was open for 0% of the time, Pallas kernels for 9%

profile of v3, /device:TPU:1, one launch (start us, length us, event | category | flops | bytes accessed | tf_op | source)
XLA Modules:
  0.0 94.4 jit_solution(9235663604250952803)
XLA Ops:
  0.6 6.6 %forward.1 = (bf16[128,40,128]{2,1,0:T(8,128)(2,1)}, s32[16,128]{1,0:T(8,128)}) custom-call(f32[8]{0:T(128)} %table_h.3, f32[128,2048]{1,0:T(8,128)} %volt_h.3, s32[128,2048]{1,0:T(8,128)} %seg_h.5, s32[16,128]{1,0:T(8,128)} %bitcast.2, s32[16,128]{1,0:T(8,128)} %bitcast.3), custom_call_target="tpu_custom_call" | custom-call | flops 268435456 | bytes 5242880 | tf_op jit(solution)/shard_map/forward/pallas_call | solution.py:347
  7.2 0.0 copy-start.5
  7.3 0.0 copy-start.6
  7.3 33.6 %all_to_all.15.got = bf16[128,40,128]{2,1,0:T(8,128)(2,1)S(1)} all-to-all(bf16[128,40,128]{2,1,0:T(8,128)(2,1)} %get-tuple-element.12), channel_id=1, replica_groups=mesh['bundle'=64,'elem'=2] {'bundle','elem'}, dimensions={0} | all-to-all | bytes 2621440 | tf_op jit(solution)/shard_map/all_to_all | solution.py:338
  40.9 0.0 copy-done.5
  40.9 0.0 copy-done.6
  40.9 3.6 %elements.1 = (f32[512,128]{1,0:T(8,128)}, bf16[128,40,128]{2,1,0:T(8,128)(2,1)S(1)}) custom-call(bf16[128,40,128]{2,1,0:T(8,128)(2,1)S(1)} %all_to_all.15.got, f32[512,128]{1,0:T(8,128)S(1)} %copy-done.5, bf16[128,128]{1,0:T(8,128)(2,1)S(1)} %copy-done.6), custom_call_target="tpu_custom_call" | custom-call | flops 2147483648 | bytes 4194304 | tf_op jit(solution)/shard_map/elements/pallas_call | solution.py:384
  44.5 0.0 copy-start.2
  44.5 1.1 %copy-done.2 = bf16[128,40,128]{2,1,0:T(8,128)(2,1)} copy-done((bf16[128,40,128]{2,1,0:T(8,128)(2,1)}, bf16[128,40,128]{2,1,0:T(8,128)(2,1)S(1)}, u32[]{:S(2)}) %copy-start.2) | copy-done | bytes 1310744
  45.6 0.0 copy-start
  45.6 0.0 copy-start.1
  45.6 0.0 copy-start.4
  45.6 4.7 %all-to-all-start.1 = ((bf16[128,40,128]{2,1,0:T(8,128)(2,1)}), bf16[128,40,128]{2,1,0:T(8,128)(2,1)S(1)}, u32[]{:S(2)}, u32[]{:S(2)}) async-start(bf16[128,40,128]{2,1,0:T(8,128)(2,1)} %copy-done.2), calls=%async_computation.1 | async-start | bytes 2621440 | tf_op jit(solution)/shard_map/all_to_all | solution.py:338
  50.3 0.0 copy-done
  50.3 0.0 copy-done.1
  50.3 0.0 copy-done.4
  50.4 0.0 copy-start.3
  50.4 8.3 %residuals.1.res_h = f32[10,128,2048]{2,1,0:T(8,128)} custom-call(f32[8]{0:T(128)S(1)} %copy-done.4, f32[128,2048]{1,0:T(8,128)S(1)} %copy-done.1, s32[128,2048]{1,0:T(8,128)S(1)} %copy-done), custom_call_target="tpu_custom_call" | custom-call | flops 268435456 | bytes 14680064 | tf_op jit(solution)/shard_map/residuals/pallas_call | solution.py:370
  58.7 13.9 %all-to-all-done.1.got = bf16[128,40,128]{2,1,0:T(8,128)(2,1)S(1)} async-done(((bf16[128,40,128]{2,1,0:T(8,128)(2,1)}), bf16[128,40,128]{2,1,0:T(8,128)(2,1)S(1)}, u32[]{:S(2)}, u32[]{:S(2)}) %all-to-all-start.1) | async-done | bytes 1310752 | tf_op jit(solution)/shard_map/all_to_all | solution.py:338
  72.5 0.0 copy-done.3
  72.5 6.9 %adjoint.1 = (f32[128,2048]{1,0:T(8,128)}, f32[128,2,128]{2,1,0:T(2,128)S(1)}) custom-call(bf16[128,40,128]{2,1,0:T(8,128)(2,1)S(1)} %all-to-all-done.1.got, s32[16,128]{1,0:T(8,128)S(1)} %copy-done.3, f32[10,128,2048]{2,1,0:T(8,128)} %residuals.1.res_h, s32[128,2048]{1,0:T(8,128)S(1)} %copy-done), custom_call_target="tpu_custom_call" | custom-call | flops 268435456 | bytes 14680064 | tf_op jit(solution)/shard_map/adjoint/pallas_call | solution.py:399
  79.5 14.2 %all_to_all.16.ends = f32[128,2,128]{2,1,0:T(2,128)S(1)} all-to-all(f32[128,2,128]{2,1,0:T(2,128)S(1)} %get-tuple-element.17), channel_id=1, replica_groups=mesh['bundle'=64,'elem'=2] {'bundle','elem'}, dimensions={0} | all-to-all | bytes 262144 | tf_op jit(solution)/shard_map/all_to_all | solution.py:338
  93.7 0.7 last_sums.1
Async XLA Ops:
  7.2 33.6 %copy-start.5 = (f32[512,128]{1,0:T(8,128)S(1)}, f32[512,128]{1,0:T(8,128)}, u32[]{:S(2)}) copy-start(f32[512,128]{1,0:T(8,128)} %cot.1) | copy-start | bytes 786436
  7.3 33.6 %copy-start.6 = (bf16[128,128]{1,0:T(8,128)(2,1)S(1)}, bf16[128,128]{1,0:T(8,128)(2,1)}, u32[]{:S(2)}) copy-start(bf16[128,128]{1,0:T(8,128)(2,1)} %material.1) | copy-start | bytes 98308
  44.5 1.1 %copy-start.2 = (bf16[128,40,128]{2,1,0:T(8,128)(2,1)}, bf16[128,40,128]{2,1,0:T(8,128)(2,1)S(1)}, u32[]{:S(2)}) copy-start(bf16[128,40,128]{2,1,0:T(8,128)(2,1)S(1)} %get-tuple-element.13) | copy-start | bytes 3932164
  45.6 4.7 %copy-start = (s32[128,2048]{1,0:T(8,128)S(1)}, s32[128,2048]{1,0:T(8,128)}, u32[]{:S(2)}) copy-start(s32[128,2048]{1,0:T(8,128)} %seg_h.5) | copy-start | bytes 3145732
  45.6 4.8 %copy-start.1 = (f32[128,2048]{1,0:T(8,128)S(1)}, f32[128,2048]{1,0:T(8,128)}, u32[]{:S(2)}) copy-start(f32[128,2048]{1,0:T(8,128)} %volt_h.3) | copy-start | bytes 3145732
  45.6 4.8 %copy-start.4 = (f32[8]{0:T(128)S(1)}, f32[8]{0:T(128)}, u32[]{:S(2)}) copy-start(f32[8]{0:T(128)} %table_h.3) | copy-start | bytes 100
  45.6 27.0 %all-to-all-start.1 = ((bf16[128,40,128]{2,1,0:T(8,128)(2,1)}), bf16[128,40,128]{2,1,0:T(8,128)(2,1)S(1)}, u32[]{:S(2)}, u32[]{:S(2)}) async-start(bf16[128,40,128]{2,1,0:T(8,128)(2,1)} %copy-done.2), calls=%async_computation.1 | async-start | bytes 2621440 | tf_op jit(solution)/shard_map/all_to_all | solution.py:338
  50.4 22.2 %copy-start.3 = (s32[16,128]{1,0:T(8,128)S(1)}, s32[16,128]{1,0:T(8,128)}, u32[]{:S(2)}) copy-start(s32[16,128]{1,0:T(8,128)} %get-tuple-element.14.slots_h) | copy-start | bytes 24580

commit v4 on v3

--- a/solution.py
+++ b/solution.py
@@ -84,42 +84,46 @@
     table_h, volt_h, seg_h, owner_h, elem_h, send, slots,
     table, volt, seg, owner, elem, act, stage, slot_s, sems, slot_sem,
 ):
-    copies = start_all(
-        [(owner_h, owner), (elem_h, elem), (table_h, table), (volt_h, volt), (seg_h, seg)], sems
+    parts = [slice(g * PART, (g + 1) * PART) for g in range(FIB // PART)]
+    small = start_all([(owner_h, owner), (elem_h, elem), (table_h, table)], sems)
+    large = start_all(
+        [(a.at[p], b.at[p]) for p in parts for a, b in ((volt_h, volt), (seg_h, seg))],
+        sems.at[3:],
     )
     stage[...] = jnp.zeros(stage.shape, F32)
-    copies[0].wait()
-    copies[1].wait()
+    for c in small + large[:2]:
+        c.wait()
 
     sub, lan = iota((LANES, LANES), 0), iota((LANES, LANES), 1)
     before = jnp.concatenate([onehot(sub < lan), jnp.ones((LANES, LANES), F32)], axis=1)
     before = before.astype(BF16)
-    sub_f = sub.astype(F32)
-    place = (sub % CAP).astype(F32)
     own_f = owner[...].astype(F32)
+    own_b = own_f.astype(BF16)
     low_f = (elem[...] & 255).astype(F32)
     high_f = ((elem[...] >> 8) + 1).astype(F32)
+    sub_b = sub.astype(F32).astype(BF16)
+    place = iota((CAP, LANES), 0).astype(F32)
     count = jnp.zeros((LANES, LANES), F32)
-    ids = jnp.zeros((2 * OWNERS, LANES), F32)
+    ids = jnp.zeros((OWNERS, 2 * CAP), F32)
     for b in range(GROUPS):
-        mine = onehot(sub_f == own_f[b : b + 1, :])
-        counted = dot(mine.astype(BF16), before)
-        rank = jnp.sum(mine * (counted[:, :LANES] + count), axis=0, keepdims=True)
+        mine = jnp.where(sub_b == own_b[b : b + 1, :], BF16(1), BF16(0))
+        counted = dot(mine, before)
+        rank = mine.astype(F32) * (counted[:, :LANES] + count)
+        rank = jnp.sum(rank, axis=0, keepdims=True)
         count = count + counted[:, LANES:]
         slots[b : b + 1, :] = (own_f[b : b + 1, :] * CAP + rank).astype(jnp.int32)
-        named = [mine * low_f[b : b + 1, :], mine * high_f[b : b + 1, :]]
-        named = jnp.concatenate(named, axis=0).astype(BF16)
-        ids = ids + dot_nt(named, onehot(place == rank).astype(BF16))
-    slot_copy = pltpu.make_async_copy(slots, slot_s, slot_sem)
-    slot_copy.start()
+        at_rank = place == rank
+        named = [jnp.where(at_rank, x[b : b + 1, :], 0.0) for x in (low_f, high_f)]
+        ids = ids + dot_nt(mine, jnp.concatenate(named, axis=0).astype(BF16))
 
     row = iota((OWNERS, 8, LANES), 1)
-    low_rows = jnp.broadcast_to(ids[:OWNERS][:, None, :], row.shape)
-    high_rows = jnp.broadcast_to(ids[OWNERS:][:, None, :], row.shape)
+    again = iota((2 * CAP, 2 * LANES), 0), iota((2 * CAP, 2 * LANES), 1)
+    again = again[0] == again[1] // LANES * CAP + again[1] % CAP
+    ids = dot(ids.astype(BF16), onehot(again).astype(BF16))
+    low_rows = jnp.broadcast_to(ids[:, None, :LANES], row.shape)
+    high_rows = jnp.broadcast_to(ids[:, None, LANES:], row.shape)
     tail = jnp.where(row == 0, low_rows, jnp.where(row == 1, high_rows, 0.0))
     send[:, CAP:, :] = tail.astype(BF16)
-    for c in copies[2:]:
-        c.wait()
 
     lane = iota((PART, LANES), 1)
 
@@ -143,10 +147,17 @@
                 stage[pl.ds(slot, 1), :] = act[f : f + 1, columns(j)]
 
     fibers(0)
-    slot_copy.wait()
+    slot_copy = pltpu.make_async_copy(slots, slot_s, slot_sem)
+    slot_copy.start()
     for g in range(1, FIB // PART):
-        scatter(g - 1)
+        for c in large[2 * g : 2 * g + 2]:
+            c.wait()
+        if g > 1:
+            scatter(g - 2)
         fibers(g)
+        if g == 1:
+            slot_copy.wait()
+    scatter(FIB // PART - 2)
     scatter(FIB // PART - 1)
     leave = []
     for m in range(CHUNKS):
@@ -245,12 +256,11 @@
 
 
 def adjoint_kernel(
-    got, slots_h, res_h, seg_h, volt_h, last,
-    rows_s, grads, sums, slot_s, seg, res, volt_grad, sems, res_sems, out_sems,
+    got, slots_h, res, seg_h, volt_h, last,
+    rows_s, grads, sums, slot_s, seg, volt_grad, sems, out_sems,
 ):
     copies = start_all([(slots_h, slot_s), (seg_h, seg)], sems)
     parts = [slice(g * PART, (g + 1) * PART) for g in range(FIB // PART)]
-    arrive = start_all([(res_h.at[:, p, :], res.at[:, p, :]) for p in parts], res_sems)
     for m in range(8):
         rows = got[16 * m : 16 * (m + 1), :CAP, :].astype(F32)
         rows_s[512 * m : 512 * (m + 1), :] = rows.reshape(512, LANES)
@@ -294,7 +304,6 @@
     gather(0)
     leave = []
     for g, p in enumerate(parts):
-        arrive[g].wait()
         if g + 1 < FIB // PART:
             gather(g + 1)
         fibers(g)
@@ -357,7 +366,7 @@
             pltpu.VMEM(fibers, F32),
             pltpu.VMEM((OWNERS * CAP, LANES), F32),
             pltpu.SMEM(index, jnp.int32),
-            pltpu.SemaphoreType.DMA((5,)),
+            pltpu.SemaphoreType.DMA((3 + 2 * (FIB // PART),)),
             pltpu.SemaphoreType.DMA,
         ],
         "forward",
@@ -380,6 +389,7 @@
         "residuals",
         1 << 28,
         14 << 20,
+        24,
     )(cond_table, volt_start, seg_ids)[0]
     stress, back = call(
         element_kernel,
@@ -398,7 +408,7 @@
     got_back = exchange(back)
     volt_grad, last = call(
         adjoint_kernel,
-        [VMEM, HBM, HBM, HBM],
+        [VMEM, HBM, VMEM, HBM],
         [(fibers, F32), ((OWNERS, 2, LANES), F32)],
         [
             pltpu.VMEM((OWNERS * CAP, LANES), F32),
@@ -406,16 +416,14 @@
             pltpu.VMEM((SEGS * 8, LANES), F32),
             pltpu.SMEM(index, jnp.int32),
             pltpu.VMEM(fibers, jnp.int32),
-            pltpu.VMEM((2 + 2 * STEPS, *fibers), F32),
             pltpu.VMEM(fibers, F32),
             pltpu.SemaphoreType.DMA((2,)),
-            pltpu.SemaphoreType.DMA((FIB // PART,)),
             pltpu.SemaphoreType.DMA((FIB // PART,)),
         ],
         "adjoint",
         1 << 28,
         14 << 20,
-        48,
+        24,
         [HBM, VMEM],
     )(got_back, slots, res, seg_ids)
     ends = exchange(last)

time: 94.7 us -> 98 us (1.035)
  local copies, waits for them, and re-layouts: 1.1 us -> 9.05 us
  Pallas kernels: 26.1 us -> 21.5 us
    unnamed x14 -> x18, local copies, waits for them, and re-layouts: 1.1 us -> 9.05 us
    pallas_call x1, Pallas kernels: 8.28 us -> 4.3 us  [per_device(): call(residual_kernel, [HBM] * 3, [((2 + 2 * STEPS, FIB, NODES), F32)], [p...]
  transfers between devices with their start and end apart: 1 -> 1, of which waited for: 1 -> 1; matrix products, arithmetic and copies ran while one was open for 0% -> 0% of each run, Pallas kernels for 9% -> 4%
where the time goes in v4:
time: 98 us; the launch traced here: 97.7 us
  blocking collectives  47.8 us (49%)
  Pallas kernels  21.5 us (22%)
  waiting for transfers between devices  13.9 us (14%)
  local copies, waits for them, and re-layouts  9.05 us (9%)
  starting transfers between devices  4.73 us (5%)
    all_to_all x2, blocking collectives, exchange(): return lax.all_to_all(x, AXES, split_axis=0, concat_axis=0, tiled=True)  47.8 us
    all_to_all x1, waiting for transfers between devices, exchange(): return lax.all_to_all(x, AXES, split_axis=0, concat_axis=0, tiled=True)  13.9 us
    unnamed x18, local copies, waits for them, and re-layouts  9.05 us
    pallas_call x1, Pallas kernels, per_device(): call(forward_kernel, [HBM] * 5, [(message, BF16), (index, jnp.int32)], [p...  6.71 us
    pallas_call x1, Pallas kernels, per_device(): call(adjoint_kernel, [VMEM, HBM, VMEM, HBM], [(fibers, F32), ((OWNERS, 2,...  6.14 us
    all_to_all x1, starting transfers between devices, exchange(): return lax.all_to_all(x, AXES, split_axis=0, concat_axis=0, tiled=True)  4.73 us
    pallas_call x1, Pallas kernels, per_device(): call(residual_kernel, [HBM] * 3, [((2 + 2 * STEPS, FIB, NODES), F32)], [p...  4.3 us
    pallas_call x1, Pallas kernels, per_device(): call(element_kernel, [VMEM] * 3, [((ELEMS, LANES), F32), (message, BF16)]...  3.62 us
  transfers between devices with their start and end apart: 1, of which 1 were waited for; matrix products, arithmetic and copies ran while one was open for 0% of the time, Pallas kernels for 4%

profile of v4, /device:TPU:1, one launch (start us, length us, event | category | flops | bytes accessed | tf_op | source)
XLA Modules:
  0.0 97.7 jit_solution(18069516146522744317)
XLA Ops:
  0.6 6.7 %forward.1 = (bf16[128,40,128]{2,1,0:T(8,128)(2,1)}, s32[16,128]{1,0:T(8,128)}) custom-call(f32[8]{0:T(128)} %table_h.3, f32[128,2048]{1,0:T(8,128)} %volt_h.3, s32[128,2048]{1,0:T(8,128)} %seg_h.5, s32[16,128]{1,0:T(8,128)} %bitcast.2, s32[16,128]{1,0:T(8,128)} %bitcast.3), custom_call_target="tpu_custom_call" | custom-call | flops 268435456 | bytes 5242880 | tf_op jit(solution)/shard_map/forward/pallas_call | solution.py:356
  7.3 0.0 copy-start.7
  7.4 0.0 copy-start.8
  7.4 33.6 %all_to_all.15.got = bf16[128,40,128]{2,1,0:T(8,128)(2,1)S(1)} all-to-all(bf16[128,40,128]{2,1,0:T(8,128)(2,1)} %get-tuple-element.12), channel_id=1, replica_groups=mesh['bundle'=64,'elem'=2] {'bundle','elem'}, dimensions={0} | all-to-all | bytes 2621440 | tf_op jit(solution)/shard_map/all_to_all | solution.py:347
  41.0 0.0 copy-done.7
  41.0 0.0 copy-done.8
  41.0 3.6 %elements.1 = (f32[512,128]{1,0:T(8,128)}, bf16[128,40,128]{2,1,0:T(8,128)(2,1)S(1)}) custom-call(bf16[128,40,128]{2,1,0:T(8,128)(2,1)S(1)} %all_to_all.15.got, f32[512,128]{1,0:T(8,128)S(1)} %copy-done.7, bf16[128,128]{1,0:T(8,128)(2,1)S(1)} %copy-done.8), custom_call_target="tpu_custom_call" | custom-call | flops 2147483648 | bytes 4194304 | tf_op jit(solution)/shard_map/elements/pallas_call | solution.py:394
  44.6 0.0 copy-start.4
  44.6 1.1 %copy-done.4 = bf16[128,40,128]{2,1,0:T(8,128)(2,1)} copy-done((bf16[128,40,128]{2,1,0:T(8,128)(2,1)}, bf16[128,40,128]{2,1,0:T(8,128)(2,1)S(1)}, u32[]{:S(2)}) %copy-start.4) | copy-done | bytes 1310744
  45.7 0.0 copy-start.2
  45.7 0.0 copy-start.3
  45.7 0.0 copy-start.6
  45.7 4.7 %all-to-all-start.1 = ((bf16[128,40,128]{2,1,0:T(8,128)(2,1)}), bf16[128,40,128]{2,1,0:T(8,128)(2,1)S(1)}, u32[]{:S(2)}, u32[]{:S(2)}) async-start(bf16[128,40,128]{2,1,0:T(8,128)(2,1)} %copy-done.4), calls=%async_computation.1 | async-start | bytes 2621440 | tf_op jit(solution)/shard_map/all_to_all | solution.py:347
  50.4 0.0 copy-done.2
  50.4 0.0 copy-done.3
  50.4 0.0 copy-done.6
  50.5 0.0 copy-start.5
  50.5 4.3 %residuals.1.res = f32[10,128,2048]{2,1,0:T(8,128)S(1)} custom-call(f32[8]{0:T(128)S(1)} %copy-done.6, f32[128,2048]{1,0:T(8,128)S(1)} %copy-done.3, s32[128,2048]{1,0:T(8,128)S(1)} %copy-done.2), custom_call_target="tpu_custom_call" | custom-call | flops 268435456 | bytes 14680064 | tf_op jit(solution)/shard_map/residuals/pallas_call | solution.py:379
  54.8 0.0 copy-start
  54.8 4.0 %copy-done = f32[10,128,2048]{2,1,0:T(8,128)} copy-done((f32[10,128,2048]{2,1,0:T(8,128)}, f32[10,128,2048]{2,1,0:T(8,128)S(1)}, u32[]{:S(2)}) %copy-start) | copy-done | bytes 10485784
  58.8 13.9 %all-to-all-done.1.got = bf16[128,40,128]{2,1,0:T(8,128)(2,1)S(1)} async-done(((bf16[128,40,128]{2,1,0:T(8,128)(2,1)}), bf16[128,40,128]{2,1,0:T(8,128)(2,1)S(1)}, u32[]{:S(2)}, u32[]{:S(2)}) %all-to-all-start.1) | async-done | bytes 1310752 | tf_op jit(solution)/shard_map/all_to_all | solution.py:347
  72.6 0.0 copy-done.5
  72.6 0.0 copy-start.1
  72.6 4.0 %copy-done.1 = f32[10,128,2048]{2,1,0:T(8,128)S(1)} copy-done((f32[10,128,2048]{2,1,0:T(8,128)S(1)}, f32[10,128,2048]{2,1,0:T(8,128)}, u32[]{:S(2)}) %copy-start.1) | copy-done | bytes 10485784
  76.6 6.1 %adjoint.1 = (f32[128,2048]{1,0:T(8,128)}, f32[128,2,128]{2,1,0:T(2,128)S(1)}) custom-call(bf16[128,40,128]{2,1,0:T(8,128)(2,1)S(1)} %all-to-all-done.1.got, s32[16,128]{1,0:T(8,128)S(1)} %copy-done.5, f32[10,128,2048]{2,1,0:T(8,128)S(1)} %copy-done.1, s32[128,2048]{1,0:T(8,128)S(1)} %copy-done.2), custom_call_target="tpu_custom_call" | custom-call | flops 268435456 | bytes 14680064 | tf_op jit(solution)/shard_map/adjoint/pallas_call | solution.py:409
  82.8 14.2 %all_to_all.16.ends = f32[128,2,128]{2,1,0:T(2,128)S(1)} all-to-all(f32[128,2,128]{2,1,0:T(2,128)S(1)} %get-tuple-element.17), channel_id=1, replica_groups=mesh['bundle'=64,'elem'=2] {'bundle','elem'}, dimensions={0} | all-to-all | bytes 262144 | tf_op jit(solution)/shard_map/all_to_all | solution.py:347
  97.0 0.7 last_sums.1
Async XLA Ops:
  7.3 33.6 %copy-start.7 = (f32[512,128]{1,0:T(8,128)S(1)}, f32[512,128]{1,0:T(8,128)}, u32[]{:S(2)}) copy-start(f32[512,128]{1,0:T(8,128)} %cot.1) | copy-start | bytes 786436
  7.4 33.6 %copy-start.8 = (bf16[128,128]{1,0:T(8,128)(2,1)S(1)}, bf16[128,128]{1,0:T(8,128)(2,1)}, u32[]{:S(2)}) copy-start(bf16[128,128]{1,0:T(8,128)(2,1)} %material.1) | copy-start | bytes 98308
  44.6 1.1 %copy-start.4 = (bf16[128,40,128]{2,1,0:T(8,128)(2,1)}, bf16[128,40,128]{2,1,0:T(8,128)(2,1)S(1)}, u32[]{:S(2)}) copy-start(bf16[128,40,128]{2,1,0:T(8,128)(2,1)S(1)} %get-tuple-element.13) | copy-start | bytes 3932164
  45.7 4.8 %copy-start.2 = (s32[128,2048]{1,0:T(8,128)S(1)}, s32[128,2048]{1,0:T(8,128)}, u32[]{:S(2)}) copy-start(s32[128,2048]{1,0:T(8,128)} %seg_h.5) | copy-start | bytes 3145732
  45.7 4.8 %copy-start.3 = (f32[128,2048]{1,0:T(8,128)S(1)}, f32[128,2048]{1,0:T(8,128)}, u32[]{:S(2)}) copy-start(f32[128,2048]{1,0:T(8,128)} %volt_h.3) | copy-start | bytes 3145732
  45.7 4.8 %copy-start.6 = (f32[8]{0:T(128)S(1)}, f32[8]{0:T(128)}, u32[]{:S(2)}) copy-start(f32[8]{0:T(128)} %table_h.3) | copy-start | bytes 100
  45.7 27.0 %all-to-all-start.1 = ((bf16[128,40,128]{2,1,0:T(8,128)(2,1)}), bf16[128,40,128]{2,1,0:T(8,128)(2,1)S(1)}, u32[]{:S(2)}, u32[]{:S(2)}) async-start(bf16[128,40,128]{2,1,0:T(8,128)(2,1)} %copy-done.4), calls=%async_computation.1 | async-start | bytes 2621440 | tf_op jit(solution)/shard_map/all_to_all | solution.py:347
  50.5 22.2 %copy-start.5 = (s32[16,128]{1,0:T(8,128)S(1)}, s32[16,128]{1,0:T(8,128)}, u32[]{:S(2)}) copy-start(s32[16,128]{1,0:T(8,128)} %get-tuple-element.14.slots_h) | copy-start | bytes 24580
  54.8 4.0 %copy-start = (f32[10,128,2048]{2,1,0:T(8,128)}, f32[10,128,2048]{2,1,0:T(8,128)S(1)}, u32[]{:S(2)}) copy-start(f32[10,128,2048]{2,1,0:T(8,128)S(1)} %residuals.1.res) | copy-start | bytes 31457284
  72.6 4.0 %copy-start.1 = (f32[10,128,2048]{2,1,0:T(8,128)S(1)}, f32[10,128,2048]{2,1,0:T(8,128)}, u32[]{:S(2)}) copy-start(f32[10,128,2048]{2,1,0:T(8,128)} %copy-done) | copy-start | bytes 31457284

commit v5 on v4

--- a/solution.py
+++ b/solution.py
@@ -166,8 +166,9 @@
         send[some, :CAP, :] = rows.reshape(-1, CAP, LANES)
 
 
-def residual_kernel(table_h, volt_h, seg_h, res, table, volt, seg, sems):
-    for c in start_all([(table_h, table), (volt_h, volt), (seg_h, seg)], sems):
+def residual_kernel(table_h, volt_h, seg_h, cot_h, res, cot, table, volt, seg, sems):
+    pairs = [(table_h, table), (volt_h, volt), (seg_h, seg), (cot_h, cot)]
+    for c in start_all(pairs, sems):
         c.wait()
     lane = iota((PART, LANES), 1)
 
@@ -256,11 +257,12 @@
 
 
 def adjoint_kernel(
-    got, slots_h, res, seg_h, volt_h, last,
-    rows_s, grads, sums, slot_s, seg, volt_grad, sems, out_sems,
+    got, slots_h, res_h, seg_h, volt_h, last,
+    rows_s, grads, sums, slot_s, seg, res, volt_grad, sems, res_sems, out_sems,
 ):
     copies = start_all([(slots_h, slot_s), (seg_h, seg)], sems)
     parts = [slice(g * PART, (g + 1) * PART) for g in range(FIB // PART)]
+    arrive = start_all([(res_h.at[:, p, :], res.at[:, p, :]) for p in parts], res_sems)
     for m in range(8):
         rows = got[16 * m : 16 * (m + 1), :CAP, :].astype(F32)
         rows_s[512 * m : 512 * (m + 1), :] = rows.reshape(512, LANES)
@@ -302,10 +304,12 @@
             sums[s * 8 : s * 8 + 8, :] = part
 
     gather(0)
+    gather(1)
     leave = []
     for g, p in enumerate(parts):
-        if g + 1 < FIB // PART:
-            gather(g + 1)
+        arrive[g].wait()
+        if g + 2 < FIB // PART:
+            gather(g + 2)
         fibers(g)
         leave += start_all([(volt_grad.at[p], volt_h.at[p])], out_sems.at[g : g + 1])
     mat = jnp.sum(got[:, CAP:, :].astype(F32), axis=0)
@@ -376,21 +380,20 @@
         [VMEM, VMEM],
     )(cond_table, volt_start, seg_ids, owner, elem)
     got = exchange(send)
-    res = call(
+    res, cot = call(
         residual_kernel,
-        [HBM] * 3,
-        [((2 + 2 * STEPS, FIB, NODES), F32)],
+        [HBM] * 4,
+        [((2 + 2 * STEPS, FIB, NODES), F32), ((ELEMS, LANES), F32)],
         [
             pltpu.SMEM((SEGS,), F32),
             pltpu.VMEM(fibers, F32),
             pltpu.VMEM(fibers, jnp.int32),
-            pltpu.SemaphoreType.DMA((3,)),
+            pltpu.SemaphoreType.DMA((4,)),
         ],
         "residuals",
         1 << 28,
         14 << 20,
-        24,
-    )(cond_table, volt_start, seg_ids)[0]
+    )(cond_table, volt_start, seg_ids, stress_cot)
     stress, back = call(
         element_kernel,
         [VMEM] * 3,
@@ -404,11 +407,11 @@
         4 << 20,
         32,
         [VMEM, VMEM],
-    )(got, stress_cot, material)
+    )(got, cot, material)
     got_back = exchange(back)
     volt_grad, last = call(
         adjoint_kernel,
-        [VMEM, HBM, VMEM, HBM],
+        [VMEM, HBM, HBM, HBM],
         [(fibers, F32), ((OWNERS, 2, LANES), F32)],
         [
             pltpu.VMEM((OWNERS * CAP, LANES), F32),
@@ -416,14 +419,16 @@
             pltpu.VMEM((SEGS * 8, LANES), F32),
             pltpu.SMEM(index, jnp.int32),
             pltpu.VMEM(fibers, jnp.int32),
+            pltpu.VMEM((2 + 2 * STEPS, *fibers), F32),
             pltpu.VMEM(fibers, F32),
             pltpu.SemaphoreType.DMA((2,)),
+            pltpu.SemaphoreType.DMA((FIB // PART,)),
             pltpu.SemaphoreType.DMA((FIB // PART,)),
         ],
         "adjoint",
         1 << 28,
         14 << 20,
-        24,
+        48,
         [HBM, VMEM],
     )(got_back, slots, res, seg_ids)
     ends = exchange(last)

time: 98 us -> 93.8 us (0.957)
  blocking collectives: 47.8 us -> 40.5 us
  starting transfers between devices: 4.73 us -> 11.5 us
  local copies, waits for them, and re-layouts: 9.05 us -> 2.62 us
  Pallas kernels: 21.5 us -> 26.1 us
  waiting for transfers between devices: 13.9 us -> 12.1 us
    all_to_all x2, blocking collectives: 47.8 us -> 40.5 us  [exchange(): return lax.all_to_all(x, AXES, split_axis=0, concat_axis=0, tiled=True)]
    all_to_all x1, starting transfers between devices: 4.73 us -> 11.5 us  [exchange(): return lax.all_to_all(x, AXES, split_axis=0, concat_axis=0, tiled=True)]
    unnamed x18 -> x16, local copies, waits for them, and re-layouts: 9.05 us -> 2.62 us
    pallas_call x2, Pallas kernels: 10.4 us -> 15 us  [the longest x1 8.3 us: per_device(): call(residual_kernel, [HBM] * 4, [((2 + 2 * STEPS, FIB, NODES), F32), ((E...]
    all_to_all x1, waiting for transfers between devices: 13.9 us -> 12.1 us  [exchange(): return lax.all_to_all(x, AXES, split_axis=0, concat_axis=0, tiled=True)]
  transfers between devices with their start and end apart: 1 -> 1, of which waited for: 1 -> 1; matrix products, arithmetic and copies ran while one was open for 0% -> 0% of each run, Pallas kernels for 4% -> 9%
where the time goes in v5:
time: 93.8 us; the launch traced here: 93.5 us
  blocking collectives  40.5 us (43%)
  Pallas kernels  26.1 us (28%)
  waiting for transfers between devices  12.1 us (13%)
  starting transfers between devices  11.5 us (12%)
  local copies, waits for them, and re-layouts  2.62 us (3%)
    all_to_all x2, blocking collectives, exchange(): return lax.all_to_all(x, AXES, split_axis=0, concat_axis=0, tiled=True)  40.5 us
    all_to_all x1, waiting for transfers between devices, exchange(): return lax.all_to_all(x, AXES, split_axis=0, concat_axis=0, tiled=True)  12.1 us
    all_to_all x1, starting transfers between devices, exchange(): return lax.all_to_all(x, AXES, split_axis=0, concat_axis=0, tiled=True)  11.5 us
    pallas_call x1, Pallas kernels, per_device(): call(residual_kernel, [HBM] * 4, [((2 + 2 * STEPS, FIB, NODES), F32), ((E...  8.3 us
    pallas_call x1, Pallas kernels, per_device(): call(adjoint_kernel, [VMEM, HBM, HBM, HBM], [(fibers, F32), ((OWNERS, 2,...  6.73 us
    pallas_call x1, Pallas kernels, per_device(): call(forward_kernel, [HBM] * 5, [(message, BF16), (index, jnp.int32)], [p...  6.7 us
    pallas_call x1, Pallas kernels, per_device(): call(element_kernel, [VMEM] * 3, [((ELEMS, LANES), F32), (message, BF16)]...  3.62 us
    unnamed x16, local copies, waits for them, and re-layouts  2.62 us
  transfers between devices with their start and end apart: 1, of which 1 were waited for; matrix products, arithmetic and copies ran while one was open for 0% of the time, Pallas kernels for 9%

profile of v5, /device:TPU:1, one launch (start us, length us, event | category | flops | bytes accessed | tf_op | source)
XLA Modules:
  0.0 93.5 jit_solution(1258209124333039738)
XLA Ops:
  0.6 6.7 %forward.1 = (bf16[128,40,128]{2,1,0:T(8,128)(2,1)}, s32[16,128]{1,0:T(8,128)}) custom-call(f32[8]{0:T(128)} %table_h.3, f32[128,2048]{1,0:T(8,128)} %volt_h.3, s32[128,2048]{1,0:T(8,128)} %seg_h.5, s32[16,128]{1,0:T(8,128)} %bitcast.2, s32[16,128]{1,0:T(8,128)} %bitcast.3), custom_call_target="tpu_custom_call" | custom-call | flops 268435456 | bytes 5242880 | tf_op jit(solution)/shard_map/forward/pallas_call | solution.py:360
  7.3 0.0 copy-start
  7.4 0.0 copy-start.1
  7.4 0.0 copy-start.4
  7.4 11.5 %all-to-all-start = ((bf16[128,40,128]{2,1,0:T(8,128)(2,1)}), bf16[128,40,128]{2,1,0:T(8,128)(2,1)S(1)}, u32[]{:S(2)}, u32[]{:S(2)}) async-start(bf16[128,40,128]{2,1,0:T(8,128)(2,1)} %get-tuple-element.14), calls=%async_computation | async-start | bytes 2621440 | tf_op jit(solution)/shard_map/all_to_all | solution.py:351
  18.9 0.0 copy-done
  18.9 0.0 copy-done.1
  18.9 0.0 copy-done.4
  18.9 0.0 copy-start.2
  18.9 0.9 %copy-done.2 = f32[512,128]{1,0:T(8,128)S(1)} copy-done((f32[512,128]{1,0:T(8,128)S(1)}, f32[512,128]{1,0:T(8,128)}, u32[]{:S(2)}) %copy-start.2) | copy-done | bytes 262168
  19.9 0.0 copy-start.7
  19.9 8.3 %residuals.1 = (f32[10,128,2048]{2,1,0:T(8,128)}, f32[512,128]{1,0:T(8,128)S(1)}) custom-call(f32[8]{0:T(128)S(1)} %copy-done.4, f32[128,2048]{1,0:T(8,128)S(1)} %copy-done.1, s32[128,2048]{1,0:T(8,128)S(1)} %copy-done, f32[512,128]{1,0:T(8,128)S(1)} %copy-done.2), custom_call_target="tpu_custom_call" | custom-call | flops 268435456 | bytes 14680064 | tf_op jit(solution)/shard_map/residuals/pallas_call | solution.py:383
  28.2 0.0 copy-start.5
  28.2 0.7 copy-done.5
  28.9 12.1 %all-to-all-done.got = bf16[128,40,128]{2,1,0:T(8,128)(2,1)S(1)} async-done(((bf16[128,40,128]{2,1,0:T(8,128)(2,1)}), bf16[128,40,128]{2,1,0:T(8,128)(2,1)S(1)}, u32[]{:S(2)}, u32[]{:S(2)}) %all-to-all-start) | async-done | bytes 1310752 | tf_op jit(solution)/shard_map/all_to_all | solution.py:351
  41.0 0.0 copy-done.7
  41.0 0.0 copy-start.6
  41.0 0.9 %copy-done.6 = f32[512,128]{1,0:T(8,128)S(1)} copy-done((f32[512,128]{1,0:T(8,128)S(1)}, f32[512,128]{1,0:T(8,128)}, u32[]{:S(2)}) %copy-start.6) | copy-done | bytes 262168
  41.9 3.6 %elements.1 = (f32[512,128]{1,0:T(8,128)}, bf16[128,40,128]{2,1,0:T(8,128)(2,1)S(1)}) custom-call(bf16[128,40,128]{2,1,0:T(8,128)(2,1)S(1)} %all-to-all-done.got, f32[512,128]{1,0:T(8,128)S(1)} %copy-done.6, bf16[128,128]{1,0:T(8,128)(2,1)S(1)} %copy-done.7), custom_call_target="tpu_custom_call" | custom-call | flops 2147483648 | bytes 4194304 | tf_op jit(solution)/shard_map/elements/pallas_call | solution.py:397
  45.6 0.0 copy-start.3
  45.6 26.3 %all_to_all.15.got = bf16[128,40,128]{2,1,0:T(8,128)(2,1)S(1)} all-to-all(bf16[128,40,128]{2,1,0:T(8,128)(2,1)S(1)} %get-tuple-element.16), channel_id=1, replica_groups=mesh['bundle'=64,'elem'=2] {'bundle','elem'}, dimensions={0} | all-to-all | bytes 2621440 | tf_op jit(solution)/shard_map/all_to_all | solution.py:351
  71.9 0.0 copy-done.3
  71.9 6.7 %adjoint.1 = (f32[128,2048]{1,0:T(8,128)}, f32[128,2,128]{2,1,0:T(2,128)S(1)}) custom-call(bf16[128,40,128]{2,1,0:T(8,128)(2,1)S(1)} %all_to_all.15.got, s32[16,128]{1,0:T(8,128)S(1)} %copy-done.3, f32[10,128,2048]{2,1,0:T(8,128)} %get-tuple-element.18.res_h, s32[128,2048]{1,0:T(8,128)S(1)} %copy-done), custom_call_target="tpu_custom_call" | custom-call | flops 268435456 | bytes 14680064 | tf_op jit(solution)/shard_map/adjoint/pallas_call | solution.py:412
  78.6 14.2 %all_to_all.16.ends = f32[128,2,128]{2,1,0:T(2,128)S(1)} all-to-all(f32[128,2,128]{2,1,0:T(2,128)S(1)} %get-tuple-element.21), channel_id=1, replica_groups=mesh['bundle'=64,'elem'=2] {'bundle','elem'}, dimensions={0} | all-to-all | bytes 262144 | tf_op jit(solution)/shard_map/all_to_all | solution.py:351
  92.8 0.7 last_sums.1
Async XLA Ops:
  7.3 11.6 %copy-start = (s32[128,2048]{1,0:T(8,128)S(1)}, s32[128,2048]{1,0:T(8,128)}, u32[]{:S(2)}) copy-start(s32[128,2048]{1,0:T(8,128)} %seg_h.5) | copy-start | bytes 3145732
  7.4 11.5 %copy-start.1 = (f32[128,2048]{1,0:T(8,128)S(1)}, f32[128,2048]{1,0:T(8,128)}, u32[]{:S(2)}) copy-start(f32[128,2048]{1,0:T(8,128)} %volt_h.3) | copy-start | bytes 3145732
  7.4 11.5 %copy-start.4 = (f32[8]{0:T(128)S(1)}, f32[8]{0:T(128)}, u32[]{:S(2)}) copy-start(f32[8]{0:T(128)} %table_h.3) | copy-start | bytes 100
  7.4 33.6 %all-to-all-start = ((bf16[128,40,128]{2,1,0:T(8,128)(2,1)}), bf16[128,40,128]{2,1,0:T(8,128)(2,1)S(1)}, u32[]{:S(2)}, u32[]{:S(2)}) async-start(bf16[128,40,128]{2,1,0:T(8,128)(2,1)} %get-tuple-element.14), calls=%async_computation | async-start | bytes 2621440 | tf_op jit(solution)/shard_map/all_to_all | solution.py:351
  18.9 1.0 %copy-start.2 = (f32[512,128]{1,0:T(8,128)S(1)}, f32[512,128]{1,0:T(8,128)}, u32[]{:S(2)}) copy-start(f32[512,128]{1,0:T(8,128)} %cot_h.1) | copy-start | bytes 786436
  19.9 21.1 %copy-start.7 = (bf16[128,128]{1,0:T(8,128)(2,1)S(1)}, bf16[128,128]{1,0:T(8,128)(2,1)}, u32[]{:S(2)}) copy-start(bf16[128,128]{1,0:T(8,128)(2,1)} %material.1) | copy-start | bytes 98308
  28.2 0.7 copy-start.5
  41.0 1.0 %copy-start.6 = (f32[512,128]{1,0:T(8,128)S(1)}, f32[512,128]{1,0:T(8,128)}, u32[]{:S(2)}) copy-start(f32[512,128]{1,0:T(8,128)} %copy-done.5) | copy-start | bytes 786436
  45.6 26.3 %copy-start.3 = (s32[16,128]{1,0:T(8,128)S(1)}, s32[16,128]{1,0:T(8,128)}, u32[]{:S(2)}) copy-start(s32[16,128]{1,0:T(8,128)} %get-tuple-element.17.slots_h) | copy-start | bytes 24580

commit v6 on v5

--- a/solution.py
+++ b/solution.py
@@ -21,6 +21,7 @@
 BF16 = jnp.bfloat16
 PART = 32
 CHUNKS = 4
+HELD = 1 << 15
 RAISE = 2.0**56
 TINY = 1e-37
 
@@ -166,8 +167,8 @@
         send[some, :CAP, :] = rows.reshape(-1, CAP, LANES)
 
 
-def residual_kernel(table_h, volt_h, seg_h, cot_h, res, cot, table, volt, seg, sems):
-    pairs = [(table_h, table), (volt_h, volt), (seg_h, seg), (cot_h, cot)]
+def residual_kernel(table_h, volt_h, seg_h, cot_h, res, held, table, volt, seg, sems):
+    pairs = [(table_h, table), (volt_h, volt), (seg_h, seg), (cot_h, held.at[:ELEMS])]
     for c in start_all(pairs, sems):
         c.wait()
     lane = iota((PART, LANES), 1)
@@ -201,7 +202,9 @@
     return high, (x - high.astype(F32)).astype(BF16)
 
 
-def element_kernel(got, cot, material, stress, back, key_row, gsum_b):
+def element_kernel(got, held, material, stress, back, cot, key_row, gsum_b, sem):
+    cot_copy = pltpu.make_async_copy(held.at[:ELEMS], cot, sem)
+    cot_copy.start()
     row = iota((OWNERS, 8, LANES), 1)
     src = iota((OWNERS, 8, LANES), 0)
     lan3 = iota((OWNERS, 8, LANES), 2)
@@ -222,6 +225,7 @@
     summed = jnp.concatenate(sums, axis=0).astype(BF16)
     out = jnp.tanh(dot(summed, material[...]))
     stress[...] = out
+    cot_copy.wait()
     gpre = cot[...] * (1.0 - out * out)
     g_high, g_low = split_two(gpre)
     raised = (dot_nt(g_high, material[...]) + dot_nt(g_low, material[...])) * RAISE
@@ -380,10 +384,10 @@
         [VMEM, VMEM],
     )(cond_table, volt_start, seg_ids, owner, elem)
     got = exchange(send)
-    res, cot = call(
+    res, held = call(
         residual_kernel,
         [HBM] * 4,
-        [((2 + 2 * STEPS, FIB, NODES), F32), ((ELEMS, LANES), F32)],
+        [((2 + 2 * STEPS, FIB, NODES), F32), ((HELD, LANES), F32)],
         [
             pltpu.SMEM((SEGS,), F32),
             pltpu.VMEM(fibers, F32),
@@ -393,21 +397,25 @@
         "residuals",
         1 << 28,
         14 << 20,
+        48,
+        [VMEM, HBM],
     )(cond_table, volt_start, seg_ids, stress_cot)
     stress, back = call(
         element_kernel,
-        [VMEM] * 3,
+        [VMEM, HBM, VMEM],
         [((ELEMS, LANES), F32), (message, BF16)],
         [
+            pltpu.VMEM((ELEMS, LANES), F32),
             pltpu.VMEM((64, LANES), F32),
             pltpu.VMEM((ELEMS, LANES), BF16),
+            pltpu.SemaphoreType.DMA,
         ],
         "elements",
         1 << 31,
         4 << 20,
-        32,
+        48,
         [VMEM, VMEM],
-    )(got, cot, material)
+    )(got, held, material)
     got_back = exchange(back)
     volt_grad, last = call(
         adjoint_kernel,

time: 93.8 us -> 92.9 us (level)
  local copies, waits for them, and re-layouts: 2.62 us -> 0.97 us
    unnamed x16 -> x12, local copies, waits for them, and re-layouts: 2.62 us -> 0.97 us
where the time goes in v6:
time: 92.9 us; the launch traced here: 92.6 us
  blocking collectives  40.5 us (44%)
  Pallas kernels  26.4 us (28%)
  waiting for transfers between devices  12.5 us (13%)
  starting transfers between devices  11.5 us (12%)
  local copies, waits for them, and re-layouts  0.97 us (1%)
    all_to_all x2, blocking collectives, exchange(): return lax.all_to_all(x, AXES, split_axis=0, concat_axis=0, tiled=True)  40.5 us
    all_to_all x1, waiting for transfers between devices, exchange(): return lax.all_to_all(x, AXES, split_axis=0, concat_axis=0, tiled=True)  12.5 us
    all_to_all x1, starting transfers between devices, exchange(): return lax.all_to_all(x, AXES, split_axis=0, concat_axis=0, tiled=True)  11.5 us
    pallas_call x1, Pallas kernels, per_device(): call(residual_kernel, [HBM] * 4, [((2 + 2 * STEPS, FIB, NODES), F32), ((H...  8.59 us
    pallas_call x1, Pallas kernels, per_device(): call(adjoint_kernel, [VMEM, HBM, HBM, HBM], [(fibers, F32), ((OWNERS, 2,...  6.73 us
    pallas_call x1, Pallas kernels, per_device(): call(forward_kernel, [HBM] * 5, [(message, BF16), (index, jnp.int32)], [p...  6.7 us
    pallas_call x1, Pallas kernels, per_device(): call(element_kernel, [VMEM, HBM, VMEM], [((ELEMS, LANES), F32), (message,...  3.69 us
  transfers between devices with their start and end apart: 1, of which 1 were waited for; matrix products, arithmetic and copies ran while one was open for 0% of the time, Pallas kernels for 9%

profile of v6, /device:TPU:1, one launch (start us, length us, event | category | flops | bytes accessed | tf_op | source)
XLA Modules:
  0.0 92.6 jit_solution(4566950311840407372)
XLA Ops:
  0.6 6.7 %forward.1 = (bf16[128,40,128]{2,1,0:T(8,128)(2,1)}, s32[16,128]{1,0:T(8,128)}) custom-call(f32[8]{0:T(128)} %table_h.3, f32[128,2048]{1,0:T(8,128)} %volt_h.3, s32[128,2048]{1,0:T(8,128)} %seg_h.5, s32[16,128]{1,0:T(8,128)} %bitcast.2, s32[16,128]{1,0:T(8,128)} %bitcast.3), custom_call_target="tpu_custom_call" | custom-call | flops 268435456 | bytes 5242880 | tf_op jit(solution)/shard_map/forward/pallas_call | solution.py:364
  7.3 0.0 copy-start
  7.4 0.0 copy-start.1
  7.4 0.0 copy-start.5
  7.4 11.5 %all-to-all-start = ((bf16[128,40,128]{2,1,0:T(8,128)(2,1)}), bf16[128,40,128]{2,1,0:T(8,128)(2,1)S(1)}, u32[]{:S(2)}, u32[]{:S(2)}) async-start(bf16[128,40,128]{2,1,0:T(8,128)(2,1)} %get-tuple-element.14), calls=%async_computation | async-start | bytes 2621440 | tf_op jit(solution)/shard_map/all_to_all | solution.py:355
  18.9 0.0 copy-done
  18.9 0.0 copy-done.1
  18.9 0.0 copy-done.5
  18.9 0.0 copy-start.2
  18.9 0.9 %copy-done.2 = f32[512,128]{1,0:T(8,128)S(1)} copy-done((f32[512,128]{1,0:T(8,128)S(1)}, f32[512,128]{1,0:T(8,128)}, u32[]{:S(2)}) %copy-start.2) | copy-done | bytes 262168
  19.9 0.0 copy-start.3
  19.9 8.6 %residuals.1 = (f32[10,128,2048]{2,1,0:T(8,128)}, f32[32768,128]{1,0:T(8,128)}) custom-call(f32[8]{0:T(128)S(1)} %copy-done.5, f32[128,2048]{1,0:T(8,128)S(1)} %copy-done.1, s32[128,2048]{1,0:T(8,128)S(1)} %copy-done, f32[512,128]{1,0:T(8,128)S(1)} %copy-done.2), custom_call_target="tpu_custom_call" | custom-call | flops 268435456 | bytes 14680064 | tf_op jit(solution)/shard_map/residuals/pallas_call | solution.py:387
  28.5 12.5 %all-to-all-done.got = bf16[128,40,128]{2,1,0:T(8,128)(2,1)S(1)} async-done(((bf16[128,40,128]{2,1,0:T(8,128)(2,1)}), bf16[128,40,128]{2,1,0:T(8,128)(2,1)S(1)}, u32[]{:S(2)}, u32[]{:S(2)}) %all-to-all-start) | async-done | bytes 1310752 | tf_op jit(solution)/shard_map/all_to_all | solution.py:355
  41.0 0.0 copy-done.3
  41.0 3.7 %elements.1 = (f32[512,128]{1,0:T(8,128)}, bf16[128,40,128]{2,1,0:T(8,128)(2,1)S(1)}) custom-call(bf16[128,40,128]{2,1,0:T(8,128)(2,1)S(1)} %all-to-all-done.got, f32[32768,128]{1,0:T(8,128)} %get-tuple-element.15.held, bf16[128,128]{1,0:T(8,128)(2,1)S(1)} %copy-done.3), custom_call_target="tpu_custom_call" | custom-call | flops 2147483648 | bytes 4194304 | tf_op jit(solution)/shard_map/elements/pallas_call | solution.py:403
  44.7 0.0 copy-start.4
  44.7 26.3 %all_to_all.15.got = bf16[128,40,128]{2,1,0:T(8,128)(2,1)S(1)} all-to-all(bf16[128,40,128]{2,1,0:T(8,128)(2,1)S(1)} %get-tuple-element.16), channel_id=1, replica_groups=mesh['bundle'=64,'elem'=2] {'bundle','elem'}, dimensions={0} | all-to-all | bytes 2621440 | tf_op jit(solution)/shard_map/all_to_all | solution.py:355
  71.0 0.0 copy-done.4
  71.0 6.7 %adjoint.1 = (f32[128,2048]{1,0:T(8,128)}, f32[128,2,128]{2,1,0:T(2,128)S(1)}) custom-call(bf16[128,40,128]{2,1,0:T(8,128)(2,1)S(1)} %all_to_all.15.got, s32[16,128]{1,0:T(8,128)S(1)} %copy-done.4, f32[10,128,2048]{2,1,0:T(8,128)} %get-tuple-element.18.res_h, s32[128,2048]{1,0:T(8,128)S(1)} %copy-done), custom_call_target="tpu_custom_call" | custom-call | flops 268435456 | bytes 14680064 | tf_op jit(solution)/shard_map/adjoint/pallas_call | solution.py:420
  77.8 14.2 %all_to_all.16.ends = f32[128,2,128]{2,1,0:T(2,128)S(1)} all-to-all(f32[128,2,128]{2,1,0:T(2,128)S(1)} %get-tuple-element.21), channel_id=1, replica_groups=mesh['bundle'=64,'elem'=2] {'bundle','elem'}, dimensions={0} | all-to-all | bytes 262144 | tf_op jit(solution)/shard_map/all_to_all | solution.py:355
  91.9 0.7 last_sums.1
Async XLA Ops:
  7.3 11.5 %copy-start = (s32[128,2048]{1,0:T(8,128)S(1)}, s32[128,2048]{1,0:T(8,128)}, u32[]{:S(2)}) copy-start(s32[128,2048]{1,0:T(8,128)} %seg_h.5) | copy-start | bytes 3145732
  7.4 11.5 %copy-start.1 = (f32[128,2048]{1,0:T(8,128)S(1)}, f32[128,2048]{1,0:T(8,128)}, u32[]{:S(2)}) copy-start(f32[128,2048]{1,0:T(8,128)} %volt_h.3) | copy-start | bytes 3145732
  7.4 11.5 %copy-start.5 = (f32[8]{0:T(128)S(1)}, f32[8]{0:T(128)}, u32[]{:S(2)}) copy-start(f32[8]{0:T(128)} %table_h.3) | copy-start | bytes 100
  7.4 33.6 %all-to-all-start = ((bf16[128,40,128]{2,1,0:T(8,128)(2,1)}), bf16[128,40,128]{2,1,0:T(8,128)(2,1)S(1)}, u32[]{:S(2)}, u32[]{:S(2)}) async-start(bf16[128,40,128]{2,1,0:T(8,128)(2,1)} %get-tuple-element.14), calls=%async_computation | async-start | bytes 2621440 | tf_op jit(solution)/shard_map/all_to_all | solution.py:355
  18.9 1.0 %copy-start.2 = (f32[512,128]{1,0:T(8,128)S(1)}, f32[512,128]{1,0:T(8,128)}, u32[]{:S(2)}) copy-start(f32[512,128]{1,0:T(8,128)} %cot_h.1) | copy-start | bytes 786436
  19.9 21.1 %copy-start.3 = (bf16[128,128]{1,0:T(8,128)(2,1)S(1)}, bf16[128,128]{1,0:T(8,128)(2,1)}, u32[]{:S(2)}) copy-start(bf16[128,128]{1,0:T(8,128)(2,1)} %material.1) | copy-start | bytes 98308
  44.7 26.3 %copy-start.4 = (s32[16,128]{1,0:T(8,128)S(1)}, s32[16,128]{1,0:T(8,128)}, u32[]{:S(2)}) copy-start(s32[16,128]{1,0:T(8,128)} %get-tuple-element.17.slots_h) | copy-start | bytes 24580

commit v7 on v6

--- a/solution.py
+++ b/solution.py
@@ -61,6 +61,32 @@
         )
         out.append(left + right)
     return out
+
+
+def split_two(x):
+    high = x.astype(BF16)
+    return high, (x - high.astype(F32)).astype(BF16)
+
+
+def stencil_weights():
+    row, col = iota((2 * LANES, 2 * LANES), 0) % LANES, iota((2 * LANES, 2 * LANES), 1)
+    inside = (jnp.abs(row - col) == 1) & (col < LANES)
+    across = (col >= LANES) & (row + col == 2 * LANES - 1)
+    across = across & ((row == 0) | (row == LANES - 1))
+    return onehot(inside | across).astype(BF16)
+
+
+def neighbour_sums(v, lane, weights):
+    size = v[0].shape[0]
+    halves = [jnp.concatenate(split_two(x), axis=1) for x in v]
+    out = dot(jnp.concatenate(halves, axis=0), weights)
+    mine = [out[j * size : (j + 1) * size, :LANES] for j in range(TILES)]
+    gives = [out[j * size : (j + 1) * size, LANES:] for j in range(TILES)]
+    first = jnp.where(lane == 0, v[0], 0.0)
+    final = jnp.where(lane == LANES - 1, v[-1], 0.0)
+    gives = [first, *gives, final]
+    low = lane < LANES // 2
+    return [mine[j] + jnp.where(low, gives[j], gives[j + 2]) for j in range(TILES)]
 
 
 def half_cond(seg, table):
@@ -160,7 +186,6 @@
             slot_copy.wait()
     scatter(FIB // PART - 2)
     scatter(FIB // PART - 1)
-    leave = []
     for m in range(CHUNKS):
         some = slice(m * OWNERS // CHUNKS, (m + 1) * OWNERS // CHUNKS)
         rows = stage[CAP * some.start : CAP * some.stop, :].astype(BF16)
@@ -197,12 +222,9 @@
     lax.fori_loop(0, FIB // PART, fibers, 0)
 
 
-def split_two(x):
-    high = x.astype(BF16)
-    return high, (x - high.astype(F32)).astype(BF16)
-
-
-def element_kernel(got, held, material, stress, back, cot, key_row, gsum_b, sem):
+def element_kernel(
+    got, held, material, stress_h, back, cot, stress, key_row, gsum_b, sem, out_sem
+):
     cot_copy = pltpu.make_async_copy(held.at[:ELEMS], cot, sem)
     cot_copy.start()
     row = iota((OWNERS, 8, LANES), 1)
@@ -225,6 +247,8 @@
     summed = jnp.concatenate(sums, axis=0).astype(BF16)
     out = jnp.tanh(dot(summed, material[...]))
     stress[...] = out
+    leave = pltpu.make_async_copy(stress, stress_h, out_sem)
+    leave.start()
     cot_copy.wait()
     gpre = cot[...] * (1.0 - out * out)
     g_high, g_low = split_two(gpre)
@@ -243,7 +267,6 @@
     diagonal = iota((LANES, LANES), 0) == iota((LANES, LANES), 1)
     weigh = jnp.where(iota((2 * LANES, LANES), 0) < LANES, 1.0, 256.0).astype(BF16)
     lane = iota((1, LANES), 1).astype(F32).astype(BF16)
-    leave = []
     for m in range(8):
         blocks = []
         for q in range(4 * m, 4 * m + 4):
@@ -258,6 +281,7 @@
         rows = dot(jnp.concatenate(hits, axis=1), gsum_b[...]).astype(BF16)
         some = slice(16 * m, 16 * m + 16)
         back[some, :CAP, :] = rows.reshape(16, CAP, LANES)
+    leave.wait()
 
 
 def adjoint_kernel(
@@ -272,6 +296,7 @@
         rows_s[512 * m : 512 * (m + 1), :] = rows.reshape(512, LANES)
     for c in copies:
         c.wait()
+    weights = stencil_weights()
     lane = iota((PART, LANES), 1)
 
     def gather(g):
@@ -293,11 +318,12 @@
             lap = cut(res[2 + k, rows, :])
             own = cut(res[2 + STEPS + k, rows, :])
             total = [t + x * d for t, x, d in zip(total, grad, lap)]
-            both = neighbours([x * y for x, y in zip(grad, c)], lane)
+            both = neighbour_sums([x * y for x, y in zip(grad, c)], lane, weights)
             grad = [x * y + z for x, y, z in zip(grad, own, both)]
         ids = cut(seg[rows, :])
         for j in range(TILES):
             volt_grad[rows, columns(j)] = grad[j]
+        leave.extend(start_all([(volt_grad.at[rows], volt_h.at[rows])], out_sems.at[g : g + 1]))
         for s in range(SEGS):
             part = jnp.where(ids[0] == s, total[0], 0.0)
             for j in range(1, TILES):
@@ -310,12 +336,11 @@
     gather(0)
     gather(1)
     leave = []
-    for g, p in enumerate(parts):
+    for g in range(FIB // PART):
         arrive[g].wait()
         if g + 2 < FIB // PART:
             gather(g + 2)
         fibers(g)
-        leave += start_all([(volt_grad.at[p], volt_h.at[p])], out_sems.at[g : g + 1])
     mat = jnp.sum(got[:, CAP:, :].astype(F32), axis=0)
     mat = jnp.sum(mat[:2, :], axis=0, keepdims=True)
     part = jnp.sum(sums[...].reshape(SEGS, 8, LANES), axis=1)
@@ -406,15 +431,17 @@
         [((ELEMS, LANES), F32), (message, BF16)],
         [
             pltpu.VMEM((ELEMS, LANES), F32),
+            pltpu.VMEM((ELEMS, LANES), F32),
             pltpu.VMEM((64, LANES), F32),
             pltpu.VMEM((ELEMS, LANES), BF16),
+            pltpu.SemaphoreType.DMA,
             pltpu.SemaphoreType.DMA,
         ],
         "elements",
         1 << 31,
         4 << 20,
         48,
-        [VMEM, VMEM],
+        [HBM, VMEM],
     )(got, held, material)
     got_back = exchange(back)
     volt_grad, last = call(

time: 92.9 us -> 92.7 us (level)
  no operation moved by 1% of the time
where the time goes in v7:
time: 92.7 us; the launch traced here: 92.5 us
  blocking collectives  40.5 us (44%)
  Pallas kernels  26.2 us (28%)
  waiting for transfers between devices  12.5 us (13%)
  starting transfers between devices  11.5 us (12%)
  local copies, waits for them, and re-layouts  0.97 us (1%)
    all_to_all x2, blocking collectives, exchange(): return lax.all_to_all(x, AXES, split_axis=0, concat_axis=0, tiled=True)  40.5 us
    all_to_all x1, waiting for transfers between devices, exchange(): return lax.all_to_all(x, AXES, split_axis=0, concat_axis=0, tiled=True)  12.5 us
    all_to_all x1, starting transfers between devices, exchange(): return lax.all_to_all(x, AXES, split_axis=0, concat_axis=0, tiled=True)  11.5 us
    pallas_call x1, Pallas kernels, per_device(): call(residual_kernel, [HBM] * 4, [((2 + 2 * STEPS, FIB, NODES), F32), ((H...  8.59 us
    pallas_call x1, Pallas kernels, per_device(): call(forward_kernel, [HBM] * 5, [(message, BF16), (index, jnp.int32)], [p...  6.7 us
    pallas_call x1, Pallas kernels, per_device(): call(adjoint_kernel, [VMEM, HBM, HBM, HBM], [(fibers, F32), ((OWNERS, 2,...  6.52 us
    pallas_call x1, Pallas kernels, per_device(): call(element_kernel, [VMEM, HBM, VMEM], [((ELEMS, LANES), F32), (message,...  3.72 us
  transfers between devices with their start and end apart: 1, of which 1 were waited for; matrix products, arithmetic and copies ran while one was open for 0% of the time, Pallas kernels for 9%

profile of v7, /device:TPU:1, one launch (start us, length us, event | category | flops | bytes accessed | tf_op | source)
XLA Modules:
  0.0 92.5 jit_solution(12900220192856117404)
XLA Ops:
  0.6 6.7 %forward.1 = (bf16[128,40,128]{2,1,0:T(8,128)(2,1)}, s32[16,128]{1,0:T(8,128)}) custom-call(f32[8]{0:T(128)} %table_h.3, f32[128,2048]{1,0:T(8,128)} %volt_h.3, s32[128,2048]{1,0:T(8,128)} %seg_h.5, s32[16,128]{1,0:T(8,128)} %bitcast.2, s32[16,128]{1,0:T(8,128)} %bitcast.3), custom_call_target="tpu_custom_call" | custom-call | flops 268435456 | bytes 5242880 | tf_op jit(solution)/shard_map/forward/pallas_call | solution.py:389
  7.3 0.0 copy-start
  7.4 0.0 copy-start.1
  7.4 0.0 copy-start.5
  7.4 11.5 %all-to-all-start = ((bf16[128,40,128]{2,1,0:T(8,128)(2,1)}), bf16[128,40,128]{2,1,0:T(8,128)(2,1)S(1)}, u32[]{:S(2)}, u32[]{:S(2)}) async-start(bf16[128,40,128]{2,1,0:T(8,128)(2,1)} %get-tuple-element.14), calls=%async_computation | async-start | bytes 2621440 | tf_op jit(solution)/shard_map/all_to_all | solution.py:380
  18.9 0.0 copy-done
  18.9 0.0 copy-done.1
  18.9 0.0 copy-done.5
  18.9 0.0 copy-start.2
  18.9 0.9 %copy-done.2 = f32[512,128]{1,0:T(8,128)S(1)} copy-done((f32[512,128]{1,0:T(8,128)S(1)}, f32[512,128]{1,0:T(8,128)}, u32[]{:S(2)}) %copy-start.2) | copy-done | bytes 262168
  19.9 0.0 copy-start.3
  19.9 8.6 %residuals.1 = (f32[10,128,2048]{2,1,0:T(8,128)}, f32[32768,128]{1,0:T(8,128)}) custom-call(f32[8]{0:T(128)S(1)} %copy-done.5, f32[128,2048]{1,0:T(8,128)S(1)} %copy-done.1, s32[128,2048]{1,0:T(8,128)S(1)} %copy-done, f32[512,128]{1,0:T(8,128)S(1)} %copy-done.2), custom_call_target="tpu_custom_call" | custom-call | flops 268435456 | bytes 14680064 | tf_op jit(solution)/shard_map/residuals/pallas_call | solution.py:412
  28.5 12.5 %all-to-all-done.got = bf16[128,40,128]{2,1,0:T(8,128)(2,1)S(1)} async-done(((bf16[128,40,128]{2,1,0:T(8,128)(2,1)}), bf16[128,40,128]{2,1,0:T(8,128)(2,1)S(1)}, u32[]{:S(2)}, u32[]{:S(2)}) %all-to-all-start) | async-done | bytes 1310752 | tf_op jit(solution)/shard_map/all_to_all | solution.py:380
  41.0 0.0 copy-done.3
  41.0 3.7 %elements.1 = (f32[512,128]{1,0:T(8,128)}, bf16[128,40,128]{2,1,0:T(8,128)(2,1)S(1)}) custom-call(bf16[128,40,128]{2,1,0:T(8,128)(2,1)S(1)} %all-to-all-done.got, f32[32768,128]{1,0:T(8,128)} %get-tuple-element.15.held, bf16[128,128]{1,0:T(8,128)(2,1)S(1)} %copy-done.3), custom_call_target="tpu_custom_call" | custom-call | flops 2147483648 | bytes 4194304 | tf_op jit(solution)/shard_map/elements/pallas_call | solution.py:428
  44.7 0.0 copy-start.4
  44.7 26.3 %all_to_all.15.got = bf16[128,40,128]{2,1,0:T(8,128)(2,1)S(1)} all-to-all(bf16[128,40,128]{2,1,0:T(8,128)(2,1)S(1)} %get-tuple-element.16), channel_id=1, replica_groups=mesh['bundle'=64,'elem'=2] {'bundle','elem'}, dimensions={0} | all-to-all | bytes 2621440 | tf_op jit(solution)/shard_map/all_to_all | solution.py:380
  71.0 0.0 copy-done.4
  71.0 6.5 %adjoint.1 = (f32[128,2048]{1,0:T(8,128)}, f32[128,2,128]{2,1,0:T(2,128)S(1)}) custom-call(bf16[128,40,128]{2,1,0:T(8,128)(2,1)S(1)} %all_to_all.15.got, s32[16,128]{1,0:T(8,128)S(1)} %copy-done.4, f32[10,128,2048]{2,1,0:T(8,128)} %get-tuple-element.18.res_h, s32[128,2048]{1,0:T(8,128)S(1)} %copy-done), custom_call_target="tpu_custom_call" | custom-call | flops 268435456 | bytes 14680064 | tf_op jit(solution)/shard_map/adjoint/pallas_call | solution.py:447
  77.6 14.2 %all_to_all.16.ends = f32[128,2,128]{2,1,0:T(2,128)S(1)} all-to-all(f32[128,2,128]{2,1,0:T(2,128)S(1)} %get-tuple-element.21), channel_id=1, replica_groups=mesh['bundle'=64,'elem'=2] {'bundle','elem'}, dimensions={0} | all-to-all | bytes 262144 | tf_op jit(solution)/shard_map/all_to_all | solution.py:380
  91.8 0.7 last_sums.1
Async XLA Ops:
  7.3 11.6 %copy-start = (s32[128,2048]{1,0:T(8,128)S(1)}, s32[128,2048]{1,0:T(8,128)}, u32[]{:S(2)}) copy-start(s32[128,2048]{1,0:T(8,128)} %seg_h.5) | copy-start | bytes 3145732
  7.4 11.5 %copy-start.1 = (f32[128,2048]{1,0:T(8,128)S(1)}, f32[128,2048]{1,0:T(8,128)}, u32[]{:S(2)}) copy-start(f32[128,2048]{1,0:T(8,128)} %volt_h.3) | copy-start | bytes 3145732
  7.4 11.5 %copy-start.5 = (f32[8]{0:T(128)S(1)}, f32[8]{0:T(128)}, u32[]{:S(2)}) copy-start(f32[8]{0:T(128)} %table_h.3) | copy-start | bytes 100
  7.4 33.6 %all-to-all-start = ((bf16[128,40,128]{2,1,0:T(8,128)(2,1)}), bf16[128,40,128]{2,1,0:T(8,128)(2,1)S(1)}, u32[]{:S(2)}, u32[]{:S(2)}) async-start(bf16[128,40,128]{2,1,0:T(8,128)(2,1)} %get-tuple-element.14), calls=%async_computation | async-start | bytes 2621440 | tf_op jit(solution)/shard_map/all_to_all | solution.py:380
  18.9 1.0 %copy-start.2 = (f32[512,128]{1,0:T(8,128)S(1)}, f32[512,128]{1,0:T(8,128)}, u32[]{:S(2)}) copy-start(f32[512,128]{1,0:T(8,128)} %cot_h.1) | copy-start | bytes 786436
  19.9 21.1 %copy-start.3 = (bf16[128,128]{1,0:T(8,128)(2,1)S(1)}, bf16[128,128]{1,0:T(8,128)(2,1)}, u32[]{:S(2)}) copy-start(bf16[128,128]{1,0:T(8,128)(2,1)} %material.1) | copy-start | bytes 98308
  44.7 26.3 %copy-start.4 = (s32[16,128]{1,0:T(8,128)S(1)}, s32[16,128]{1,0:T(8,128)}, u32[]{:S(2)}) copy-start(s32[16,128]{1,0:T(8,128)} %get-tuple-element.17.slots_h) | copy-start | bytes 24580

commit v8 on v7

--- a/solution.py
+++ b/solution.py
@@ -118,7 +118,7 @@
         sems.at[3:],
     )
     stage[...] = jnp.zeros(stage.shape, F32)
-    for c in small + large[:2]:
+    for c in small[:2]:
         c.wait()
 
     sub, lan = iota((LANES, LANES), 0), iota((LANES, LANES), 1)
@@ -151,6 +151,8 @@
     high_rows = jnp.broadcast_to(ids[:, None, LANES:], row.shape)
     tail = jnp.where(row == 0, low_rows, jnp.where(row == 1, high_rows, 0.0))
     send[:, CAP:, :] = tail.astype(BF16)
+    for c in small[2:] + large[:2]:
+        c.wait()
 
     lane = iota((PART, LANES), 1)
 
@@ -294,8 +296,7 @@
     for m in range(8):
         rows = got[16 * m : 16 * (m + 1), :CAP, :].astype(F32)
         rows_s[512 * m : 512 * (m + 1), :] = rows.reshape(512, LANES)
-    for c in copies:
-        c.wait()
+    copies[0].wait()
     weights = stencil_weights()
     lane = iota((PART, LANES), 1)
 
@@ -336,6 +337,7 @@
     gather(0)
     gather(1)
     leave = []
+    copies[1].wait()
     for g in range(FIB // PART):
         arrive[g].wait()
         if g + 2 < FIB // PART:

time: 92.7 us -> 93 us (level)
  no operation moved by 1% of the time
where the time goes in v8:
time: 93 us; the launch traced here: 92.7 us
  blocking collectives  40.5 us (44%)
  Pallas kernels  26.5 us (28%)
  waiting for transfers between devices  12.5 us (13%)
  starting transfers between devices  11.5 us (12%)
  local copies, waits for them, and re-layouts  0.97 us (1%)
    all_to_all x2, blocking collectives, exchange(): return lax.all_to_all(x, AXES, split_axis=0, concat_axis=0, tiled=True)  40.5 us
    all_to_all x1, waiting for transfers between devices, exchange(): return lax.all_to_all(x, AXES, split_axis=0, concat_axis=0, tiled=True)  12.5 us
    all_to_all x1, starting transfers between devices, exchange(): return lax.all_to_all(x, AXES, split_axis=0, concat_axis=0, tiled=True)  11.5 us
    pallas_call x1, Pallas kernels, per_device(): call(residual_kernel, [HBM] * 4, [((2 + 2 * STEPS, FIB, NODES), F32), ((H...  8.59 us
    pallas_call x1, Pallas kernels, per_device(): call(forward_kernel, [HBM] * 5, [(message, BF16), (index, jnp.int32)], [p...  6.97 us
    pallas_call x1, Pallas kernels, per_device(): call(adjoint_kernel, [VMEM, HBM, HBM, HBM], [(fibers, F32), ((OWNERS, 2,...  6.53 us
    pallas_call x1, Pallas kernels, per_device(): call(element_kernel, [VMEM, HBM, VMEM], [((ELEMS, LANES), F32), (message,...  3.73 us
  transfers between devices with their start and end apart: 1, of which 1 were waited for; matrix products, arithmetic and copies ran while one was open for 0% of the time, Pallas kernels for 9%

profile of v8, /device:TPU:1, one launch (start us, length us, event | category | flops | bytes accessed | tf_op | source)
XLA Modules:
  0.0 92.7 jit_solution(10814115308790225157)
XLA Ops:
  0.6 7.0 %forward.1 = (bf16[128,40,128]{2,1,0:T(8,128)(2,1)}, s32[16,128]{1,0:T(8,128)}) custom-call(f32[8]{0:T(128)} %table_h.3, f32[128,2048]{1,0:T(8,128)} %volt_h.3, s32[128,2048]{1,0:T(8,128)} %seg_h.5, s32[16,128]{1,0:T(8,128)} %bitcast.2, s32[16,128]{1,0:T(8,128)} %bitcast.3), custom_call_target="tpu_custom_call" | custom-call | flops 268435456 | bytes 5242880 | tf_op jit(solution)/shard_map/forward/pallas_call | solution.py:391
  7.6 0.0 copy-start
  7.6 0.0 copy-start.1
  7.6 0.0 copy-start.5
  7.6 11.5 %all-to-all-start = ((bf16[128,40,128]{2,1,0:T(8,128)(2,1)}), bf16[128,40,128]{2,1,0:T(8,128)(2,1)S(1)}, u32[]{:S(2)}, u32[]{:S(2)}) async-start(bf16[128,40,128]{2,1,0:T(8,128)(2,1)} %get-tuple-element.14), calls=%async_computation | async-start | bytes 2621440 | tf_op jit(solution)/shard_map/all_to_all | solution.py:382
  19.2 0.0 copy-done
  19.2 0.0 copy-done.1
  19.2 0.0 copy-done.5
  19.2 0.0 copy-start.2
  19.2 0.9 %copy-done.2 = f32[512,128]{1,0:T(8,128)S(1)} copy-done((f32[512,128]{1,0:T(8,128)S(1)}, f32[512,128]{1,0:T(8,128)}, u32[]{:S(2)}) %copy-start.2) | copy-done | bytes 262168
  20.1 0.0 copy-start.3
  20.1 8.6 %residuals.1 = (f32[10,128,2048]{2,1,0:T(8,128)}, f32[32768,128]{1,0:T(8,128)}) custom-call(f32[8]{0:T(128)S(1)} %copy-done.5, f32[128,2048]{1,0:T(8,128)S(1)} %copy-done.1, s32[128,2048]{1,0:T(8,128)S(1)} %copy-done, f32[512,128]{1,0:T(8,128)S(1)} %copy-done.2), custom_call_target="tpu_custom_call" | custom-call | flops 268435456 | bytes 14680064 | tf_op jit(solution)/shard_map/residuals/pallas_call | solution.py:414
  28.7 12.5 %all-to-all-done.got = bf16[128,40,128]{2,1,0:T(8,128)(2,1)S(1)} async-done(((bf16[128,40,128]{2,1,0:T(8,128)(2,1)}), bf16[128,40,128]{2,1,0:T(8,128)(2,1)S(1)}, u32[]{:S(2)}, u32[]{:S(2)}) %all-to-all-start) | async-done | bytes 1310752 | tf_op jit(solution)/shard_map/all_to_all | solution.py:382
  41.2 0.0 copy-done.3
  41.2 3.7 %elements.1 = (f32[512,128]{1,0:T(8,128)}, bf16[128,40,128]{2,1,0:T(8,128)(2,1)S(1)}) custom-call(bf16[128,40,128]{2,1,0:T(8,128)(2,1)S(1)} %all-to-all-done.got, f32[32768,128]{1,0:T(8,128)} %get-tuple-element.15.held, bf16[128,128]{1,0:T(8,128)(2,1)S(1)} %copy-done.3), custom_call_target="tpu_custom_call" | custom-call | flops 2147483648 | bytes 4194304 | tf_op jit(solution)/shard_map/elements/pallas_call | solution.py:430
  45.0 0.0 copy-start.4
  45.0 26.3 %all_to_all.15.got = bf16[128,40,128]{2,1,0:T(8,128)(2,1)S(1)} all-to-all(bf16[128,40,128]{2,1,0:T(8,128)(2,1)S(1)} %get-tuple-element.16), channel_id=1, replica_groups=mesh['bundle'=64,'elem'=2] {'bundle','elem'}, dimensions={0} | all-to-all | bytes 2621440 | tf_op jit(solution)/shard_map/all_to_all | solution.py:382
  71.3 0.0 copy-done.4
  71.3 6.5 %adjoint.1 = (f32[128,2048]{1,0:T(8,128)}, f32[128,2,128]{2,1,0:T(2,128)S(1)}) custom-call(bf16[128,40,128]{2,1,0:T(8,128)(2,1)S(1)} %all_to_all.15.got, s32[16,128]{1,0:T(8,128)S(1)} %copy-done.4, f32[10,128,2048]{2,1,0:T(8,128)} %get-tuple-element.18.res_h, s32[128,2048]{1,0:T(8,128)S(1)} %copy-done), custom_call_target="tpu_custom_call" | custom-call | flops 268435456 | bytes 14680064 | tf_op jit(solution)/shard_map/adjoint/pallas_call | solution.py:449
  77.8 14.2 %all_to_all.16.ends = f32[128,2,128]{2,1,0:T(2,128)S(1)} all-to-all(f32[128,2,128]{2,1,0:T(2,128)S(1)} %get-tuple-element.21), channel_id=1, replica_groups=mesh['bundle'=64,'elem'=2] {'bundle','elem'}, dimensions={0} | all-to-all | bytes 262144 | tf_op jit(solution)/shard_map/all_to_all | solution.py:382
  92.0 0.7 last_sums.1
Async XLA Ops:
  7.6 11.5 %copy-start = (s32[128,2048]{1,0:T(8,128)S(1)}, s32[128,2048]{1,0:T(8,128)}, u32[]{:S(2)}) copy-start(s32[128,2048]{1,0:T(8,128)} %seg_h.5) | copy-start | bytes 3145732
  7.6 11.5 %copy-start.1 = (f32[128,2048]{1,0:T(8,128)S(1)}, f32[128,2048]{1,0:T(8,128)}, u32[]{:S(2)}) copy-start(f32[128,2048]{1,0:T(8,128)} %volt_h.3) | copy-start | bytes 3145732
  7.6 11.5 %copy-start.5 = (f32[8]{0:T(128)S(1)}, f32[8]{0:T(128)}, u32[]{:S(2)}) copy-start(f32[8]{0:T(128)} %table_h.3) | copy-start | bytes 100
  7.6 33.6 %all-to-all-start = ((bf16[128,40,128]{2,1,0:T(8,128)(2,1)}), bf16[128,40,128]{2,1,0:T(8,128)(2,1)S(1)}, u32[]{:S(2)}, u32[]{:S(2)}) async-start(bf16[128,40,128]{2,1,0:T(8,128)(2,1)} %get-tuple-element.14), calls=%async_computation | async-start | bytes 2621440 | tf_op jit(solution)/shard_map/all_to_all | solution.py:382
  19.2 1.0 %copy-start.2 = (f32[512,128]{1,0:T(8,128)S(1)}, f32[512,128]{1,0:T(8,128)}, u32[]{:S(2)}) copy-start(f32[512,128]{1,0:T(8,128)} %cot_h.1) | copy-start | bytes 786436
  20.1 21.1 %copy-start.3 = (bf16[128,128]{1,0:T(8,128)(2,1)S(1)}, bf16[128,128]{1,0:T(8,128)(2,1)}, u32[]{:S(2)}) copy-start(bf16[128,128]{1,0:T(8,128)(2,1)} %material.1) | copy-start | bytes 98308
  45.0 26.3 %copy-start.4 = (s32[16,128]{1,0:T(8,128)S(1)}, s32[16,128]{1,0:T(8,128)}, u32[]{:S(2)}) copy-start(s32[16,128]{1,0:T(8,128)} %get-tuple-element.17.slots_h) | copy-start | bytes 24580
